TPU v7x, 32 devices: a whole 2x2x4 slice. The times are simulated.
32 devices in a mesh: seq: 8 (over z, x), ch: 4 (over y, core).
Axes of the slice: x: 2, y: 2, z: 4, core: 2. Of those that a mesh axis runs over, the one named last changes fastest.
Arguments:
- proj: bfloat16 [3, 128, 8192], P(None, 'ch', 'seq'), may hold values from -6 to 6
- cotangent: bfloat16 [128, 8192], P('ch', 'seq'), may hold values from -6 to 6
- short_w: float32 [3, 128, 3], P(None, 'ch'), may hold values from -3.5 to 3.5
- filter_in: float32 [32, 64], replicated, may hold values from -5 to 5
- filter_out: float32 [64, 128], P(None, 'ch'), may hold values from -0.75 to 0.75
- rates: float32 [128], P('ch'), may hold values from 0.25 to 273
Outputs:
- grad_proj: bfloat16 [3, 128, 8192], P(None, 'ch', 'seq')
- grad_short: float32 [3, 128, 3], P(None, 'ch')
- grad_filter_out: float32 [64, 128], P(None, 'ch')
- grad_filter_in: float32 [32, 64], replicated
All inputs are finite; a program needn't handle non-finite values.
Results may differ from a plain program's by a relative error of at most 0.0013.
Values may be sent and summed in bfloat16 or wider, within the bound.
No kernel may reach another device: no remote copies, remote signals or barrier semaphores. Data moves between devices by JAX's collectives and lax.ppermute only.
A program may use at most 64 MiB of HBM per device.

v0:
```python
import functools
import math

import jax
import jax.numpy as jnp
import ml_dtypes
import numpy as np
from jax import lax
from jax.experimental import pallas as pl
from jax.experimental.pallas import tpu as pltpu
from jax.sharding import PartitionSpec as P

F32 = jnp.float32
BF16 = jnp.bfloat16
LANES = 128
VMEM_BYTES = 56 * 1024 * 1024


def split(value):
    high = value.astype(BF16)
    return high, (value - high.astype(F32)).astype(BF16)


def split_outside(value):
    high = lax.reduce_precision(value, 8, 7)
    return high.astype(BF16), (value - high).astype(BF16)


def np_split(value):
    high = value.astype(ml_dtypes.bfloat16)
    return high, (value - high.astype(np.float64)).astype(ml_dtypes.bfloat16)


def dot(left, right):
    return jnp.dot(left, right, preferred_element_type=F32)


def dot_last(left, right):
    return lax.dot_general(left, right, (((1,), (1,)), ((), ())), preferred_element_type=F32)


@functools.lru_cache(maxsize=None)
def transform_tables(length):
    rows = length // LANES
    points = 2 * length
    lows = rows + 8
    low = np.arange(lows)
    row = np.arange(rows)
    lane = np.arange(LANES)
    angle = 2.0 * np.pi * ((low[:, None] * row[None, :]) % (2 * rows)) / (2 * rows)
    kept = (low <= rows)[:, None]
    first = np.concatenate([np.cos(angle) * kept, -np.sin(angle) * kept], 0)
    weight = np.where((low == 0) | (low == rows), 1.0, 2.0)[:, None] / points
    last = np.concatenate([np.cos(angle) * kept * weight, -np.sin(angle) * kept * weight], 0).T
    turn = 2.0 * np.pi * ((low[:, None] * lane[None, :]) % points) / points
    lane_angle = 2.0 * np.pi * ((lane[:, None] * lane[None, :]) % LANES) / LANES
    cosine, sine = np.cos(lane_angle), np.sin(lane_angle)
    middle = np.block([[cosine, -sine], [sine, cosine]])
    first_high, first_low = np_split(first)
    last_high, last_low = np_split(last)
    middle_high, middle_low = np_split(middle)
    return dict(
        first=np.concatenate([first_high, first_high, first_low], 1),
        last=np.concatenate([last_high, last_high, last_low], 1),
        middle=np.concatenate([middle_high, middle_low], 0),
        turn=np.concatenate([np.cos(turn), np.sin(turn)], 0).astype(np.float32),
    )


@functools.lru_cache(maxsize=None)
def feature_tables(length, feature_count):
    rows = length // LANES
    feature = np.arange(feature_count)
    multiplier = (1 + feature // 2 * 499) % length
    row_angle = 2.0 * np.pi * ((multiplier[:, None] * LANES * np.arange(rows)[None, :]) % length) / length
    lane_angle = 2.0 * np.pi * ((multiplier[:, None] * np.arange(LANES)[None, :]) % length) / length
    even = (feature % 2 == 0)[:, None]
    near = np.where(even, np.cos(row_angle), np.sin(row_angle))
    far = np.where(even, -np.sin(row_angle), np.cos(row_angle))
    return (
        np.concatenate([near, far], 0).astype(np.float32),
        np.concatenate([np.cos(lane_angle), np.sin(lane_angle)], 0).astype(np.float32),
    )


def middle_dot(value, middle_ref):
    high, low = split(value)
    size = 2 * LANES
    table_high, table_low = middle_ref[:size, :], middle_ref[size:, :]
    return dot(high, table_high) + dot(high, table_low) + dot(low, table_high)


def forward(signals, first_ref, middle_ref, turn_ref):
    lows = turn_ref.shape[0] // 2
    high, low = split(jnp.concatenate(signals, 1))
    partial = dot(first_ref[...], jnp.concatenate([high, low, high], 0))
    cosine, sine = turn_ref[:lows, :], turn_ref[lows:, :]
    turned = []
    for index in range(len(signals)):
        real = partial[:lows, index * LANES : (index + 1) * LANES]
        imag = partial[lows:, index * LANES : (index + 1) * LANES]
        turned.append(
            jnp.concatenate([real * cosine + imag * sine, imag * cosine - real * sine], 1)
        )
    return middle_dot(jnp.concatenate(turned, 0), middle_ref)


def backward(spectra, last_ref, middle_ref, turn_ref):
    lows = turn_ref.shape[0] // 2
    swapped = jnp.concatenate([jnp.concatenate([imag, real], 1) for real, imag in spectra], 0)
    partial = middle_dot(swapped, middle_ref)
    cosine, sine = turn_ref[:lows, :], turn_ref[lows:, :]
    turned = []
    for index in range(len(spectra)):
        imag = partial[index * lows : (index + 1) * lows, :LANES]
        real = partial[index * lows : (index + 1) * lows, LANES:]
        turned.append(
            jnp.concatenate([real * cosine - imag * sine, imag * cosine + real * sine], 0)
        )
    high, low = split(jnp.concatenate(turned, 1))
    result = dot(last_ref[...], jnp.concatenate([high, low, high], 0))
    return [result[:, index * LANES : (index + 1) * LANES] for index in range(len(spectra))]


def later(value):
    turned = pltpu.roll(value, 1, 1)
    carried = pltpu.roll(turned, 1, 0)
    row = lax.broadcasted_iota(jnp.int32, value.shape, 0)
    lane = lax.broadcasted_iota(jnp.int32, value.shape, 1)
    carried = jnp.where(row == 0, 0.0, carried)
    return jnp.where(lane == 0, carried, turned)


def sooner(value):
    rows = value.shape[0]
    turned = pltpu.roll(value, LANES - 1, 1)
    carried = pltpu.roll(turned, rows - 1, 0)
    row = lax.broadcasted_iota(jnp.int32, value.shape, 0)
    lane = lax.broadcasted_iota(jnp.int32, value.shape, 1)
    carried = jnp.where(row == rows - 1, 0.0, carried)
    return jnp.where(lane == LANES - 1, carried, turned)


def sine_cosine(angle):
    turns = jnp.round(angle * (1.0 / math.pi))
    rest = angle - turns * 3.140625
    rest = rest - turns * 9.67502593994140625e-4
    rest = rest - turns * 1.509957990978376432e-7
    half = turns * 0.5
    sign = 1.0 - 4.0 * jnp.abs(half - jnp.round(half))
    square = rest * rest
    sine = -1.0 / 39916800.0
    for coefficient in (1.0 / 362880.0, -1.0 / 5040.0, 1.0 / 120.0, -1.0 / 6.0, 1.0):
        sine = sine * square + coefficient
    cosine = 1.0 / 479001600.0
    for coefficient in (-1.0 / 3628800.0, 1.0 / 40320.0, -1.0 / 720.0, 1.0 / 24.0, -0.5, 1.0):
        cosine = cosine * square + coefficient
    return sine * (rest * sign), cosine * sign


def pack_kernel(per, proj_ref, cot_ref, out_ref):
    channels = cot_ref.shape[0]
    whole = [proj_ref[index].astype(F32) for index in range(3)] + [cot_ref[...].astype(F32)]
    for device in range(out_ref.shape[0]):
        start = device * per % channels
        rows = jnp.concatenate([part[start : start + per, :] for part in whole], 0)
        out_ref[device] = rows.astype(BF16)


def block_features(near_ref, lane_ref):
    count = lane_ref.shape[0] // 2
    lane_cos, lane_sin = lane_ref[:count, :], lane_ref[count:, :]
    near, far = near_ref[0, :count, :], near_ref[0, count:, :]
    rows = range(near_ref.shape[2])
    blocks = [near[:, row : row + 1] * lane_cos + far[:, row : row + 1] * lane_sin for row in rows]
    return split(jnp.concatenate(blocks, 1))


def hidden_kernel(
    near_ref, lane_ref, in_ref, out_ref, sine_high_ref, sine_low_ref, cosine_ref, mod_ref
):
    high, low = block_features(near_ref, lane_ref)
    preact = dot(in_ref[...], jnp.concatenate([high, low, high], 0))
    sine, cosine = sine_cosine(preact)
    cosine_ref[...] = cosine
    high, low = split(sine)
    sine_high_ref[...] = high
    sine_low_ref[...] = low
    mod_ref[...] = dot(out_ref[...], jnp.concatenate([high, low, high], 0))


def filter_kernel(
    per, length, rates_ref, scale_ref, mod_ref, first_ref, middle_ref, turn_ref, env_ref, spec_ref, stage_ref
):
    rows = length // LANES
    for row in range(rows):
        stage_ref[row * 8 : (row + 1) * 8, :] = mod_ref[:, row * LANES : (row + 1) * LANES]
    position = lax.broadcasted_iota(jnp.int32, (rows, LANES), 0) * LANES
    position = position + lax.broadcasted_iota(jnp.int32, (rows, LANES), 1)
    relative = position.astype(F32) * (1.0 / length)
    kernels = []
    for channel in range(per):
        envelope = jnp.exp(-rates_ref[channel] * relative) * scale_ref[channel]
        env_ref[channel * rows : (channel + 1) * rows, :] = envelope
        kernels.append(envelope * stage_ref[pl.ds(channel, rows, stride=8), :])
    spec_ref[...] = forward(kernels, first_ref, middle_ref, turn_ref)


def spectra_kernel(
    per,
    short_ref,
    recv_ref,
    env_ref,
    first_ref,
    last_ref,
    middle_ref,
    turn_ref,
    raw_ref,
    mixed_ref,
    spec_ref,
    weighted_ref,
    stage_ref,
):
    devices, held, tokens = recv_ref.shape
    step = raw_ref.shape[0] // (devices * tokens // LANES)
    rows = devices * tokens // LANES
    lows = turn_ref.shape[0] // 2
    for device in range(devices):
        for part in range(tokens // LANES):
            at = (device * (tokens // LANES) + part) * step
            raw_ref[at : at + held, :] = recv_ref[
                device, :, part * LANES : (part + 1) * LANES
            ].astype(F32)
    gated, grads = [], []
    for channel in range(per):
        mixed = []
        for index in range(3):
            base = raw_ref[pl.ds(index * per + channel, rows, stride=step), :]
            total = short_ref[(index * per + channel) * 3] * base
            for tap in (1, 2):
                base = later(base)
                total = total + short_ref[(index * per + channel) * 3 + tap] * base
            mixed.append(total)
        cotangent = raw_ref[pl.ds(3 * per + channel, rows, stride=step), :]
        mixed_ref[2 * channel] = mixed[1]
        mixed_ref[2 * channel + 1] = mixed[2]
        gated.append(mixed[1] * mixed[2])
        grads.append(cotangent * mixed[0])
    spectra = forward(gated + grads, first_ref, middle_ref, turn_ref)
    spec_ref[...] = spectra
    products = []
    for channel in range(per):
        at, other = channel * lows, (per + channel) * lows
        gated_real, gated_imag = spectra[at : at + lows, :LANES], spectra[at : at + lows, LANES:]
        grad_real, grad_imag = (
            spectra[other : other + lows, :LANES],
            spectra[other : other + lows, LANES:],
        )
        products.append(
            (
                grad_real * gated_real + grad_imag * gated_imag,
                grad_imag * gated_real - grad_real * gated_imag,
            )
        )
    results = backward(products, last_ref, middle_ref, turn_ref)
    if per < 8:
        stage_ref[...] = jnp.zeros_like(stage_ref)
    for channel in range(per):
        weighted = results[channel] * env_ref[channel * rows : (channel + 1) * rows, :]
        stage_ref[pl.ds(channel, rows, stride=8), :] = weighted
    for row in range(rows):
        weighted_ref[:, row * LANES : (row + 1) * LANES] = stage_ref[row * 8 : (row + 1) * 8, :]


def filter_grad_kernel(
    weighted_ref,
    sine_high_ref,
    sine_low_ref,
    cosine_ref,
    near_ref,
    lane_ref,
    fo_ref,
    out_grad_ref,
    in_grad_ref,
):
    count = lane_ref.shape[0] // 2
    feature_high, feature_low = block_features(near_ref, lane_ref)
    high, low = split(weighted_ref[...])
    both = jnp.concatenate([weighted_ref[...], weighted_ref[...] - high.astype(F32)], 0).astype(BF16)
    first = dot_last(both, sine_high_ref[...])
    out_grad = first[:8] + first[8:] + dot_last(high, sine_low_ref[...])
    grad = dot(fo_ref[...], jnp.concatenate([both.astype(F32), high.astype(F32)], 0).astype(BF16))
    grad_high, grad_low = split(grad * cosine_ref[...])
    second = dot_last(jnp.concatenate([feature_high, feature_low], 0), grad_high)
    in_grad = second[:count] + second[count:] + dot_last(feature_high, grad_low)

    @pl.when(pl.program_id(0) == 0)
    def _():
        out_grad_ref[...] = jnp.zeros_like(out_grad_ref)
        in_grad_ref[...] = jnp.zeros_like(in_grad_ref)

    out_grad_ref[...] += out_grad
    in_grad_ref[...] += in_grad


def proj_grad_kernel(
    per,
    scale,
    short_ref,
    raw_ref,
    mixed_ref,
    spec_ref,
    kernel_spec_ref,
    out_grad_ref,
    last_ref,
    middle_ref,
    turn_ref,
    slab_ref,
    stage_ref,
):
    devices, held, width = slab_ref.shape
    tokens = width - 3 * LANES
    rows = devices * tokens // LANES
    step = raw_ref.shape[0] // rows
    lows = turn_ref.shape[0] // 2
    products = []
    for sign in (1.0, -1.0):
        for channel in range(per):
            at = (channel if sign > 0 else per + channel) * lows
            real, imag = spec_ref[at : at + lows, :LANES], spec_ref[at : at + lows, LANES:]
            at = channel * lows
            kernel_real = kernel_spec_ref[at : at + lows, :LANES]
            kernel_imag = sign * kernel_spec_ref[at : at + lows, LANES:]
            products.append(
                (
                    real * kernel_real - imag * kernel_imag,
                    real * kernel_imag + imag * kernel_real,
                )
            )
    results = backward(products, last_ref, middle_ref, turn_ref)
    sums = [None] * (3 * per)
    for channel in range(per):
        cotangent = raw_ref[pl.ds(3 * per + channel, rows, stride=step), :]
        grad_mixed = (
            cotangent * results[channel],
            results[per + channel] * mixed_ref[2 * channel + 1],
            results[per + channel] * mixed_ref[2 * channel],
        )
        for index in range(3):
            base = raw_ref[pl.ds(index * per + channel, rows, stride=step), :]
            grad = grad_mixed[index]
            total = short_ref[(index * per + channel) * 3] * grad
            taps = [jnp.sum(grad * base, axis=0, keepdims=True)]
            moved = grad
            for tap in (1, 2):
                base = later(base)
                moved = sooner(moved)
                total = total + short_ref[(index * per + channel) * 3 + tap] * moved
                taps.append(jnp.sum(grad * base, axis=0, keepdims=True))
            sums[index * per + channel] = jnp.concatenate(taps, 0)
            stage_ref[pl.ds(index * per + channel, rows, stride=held), :] = total
    for device in range(devices):
        for part in range(tokens // LANES):
            at = (device * (tokens // LANES) + part) * held
            slab_ref[device, :, part * LANES : (part + 1) * LANES] = stage_ref[
                at : at + held, :
            ].astype(BF16)
    row = lax.broadcasted_iota(jnp.int32, (held, LANES), 0)
    lane = lax.broadcasted_iota(jnp.int32, (held, LANES), 1)
    small = jnp.zeros((held, LANES), F32)
    for place in range(3 * per):
        taps = jnp.sum(sums[place], axis=1, keepdims=True) * scale
        for tap in range(3):
            small = jnp.where((row == 4 + place) & (lane == tap), taps[tap : tap + 1, :], small)
    order = out_grad_ref.shape[1]
    out_grad = jnp.concatenate(
        [out_grad_ref[...] * scale, jnp.zeros((8, LANES - order), F32)], 1
    )
    out_grad = jnp.concatenate([out_grad, jnp.zeros((held - 8, LANES), F32)], 0)
    small = jnp.where(row < per, out_grad, small)
    rest = pltpu.roll(small - small.astype(BF16).astype(F32), LANES // 2, 1)
    small = jnp.where(lane < LANES // 2, small, rest).astype(BF16)
    for device in range(devices):
        slab_ref[device, :, tokens : tokens + LANES] = small


def unpack_kernel(per, recv_ref, proj_ref, short_ref, out_ref, in_ref):
    channels, tokens = proj_ref.shape[1:]
    devices = channels // per
    order = out_ref.shape[0]
    for index in range(3):
        rows = [
            recv_ref[device, index * per : (index + 1) * per, :tokens].astype(F32)
            for device in range(devices)
        ]
        proj_ref[index] = jnp.concatenate(rows, 0).astype(BF16)
    small = [recv_ref[device, :, tokens : tokens + LANES].astype(F32) for device in range(devices)]
    small = [part + pltpu.roll(part, LANES // 2, 1) for part in small]
    for index in range(3):
        at = 4 + index * per
        short_ref[index] = jnp.concatenate([part[at : at + per, :3] for part in small], 0)
    out_grad = jnp.concatenate([part[:per, :] for part in small], 0)
    out_ref[...] = out_grad.T[:order, :]
    extra = [
        recv_ref[device, :, tokens + LANES :].astype(F32) for device in range(devices)
    ]
    total = functools.reduce(lambda a, b: a + b, extra)
    total = jnp.concatenate([total[:, :LANES], total[:, LANES:]], 0)
    in_ref[...] = total[:, :order] + total[:, order:]


def call(kernel, out, grid=None, in_specs=None, out_specs=None, scratch=(), flops=0, moved=0):
    vmem = pl.BlockSpec(memory_space=pltpu.VMEM)
    extra = {}
    if grid is not None:
        extra = dict(grid=grid)
    return pl.pallas_call(
        kernel,
        out_shape=out,
        in_specs=in_specs,
        out_specs=out_specs if out_specs is not None else jax.tree.map(lambda _: vmem, out),
        scratch_shapes=scratch,
        compiler_params=pltpu.CompilerParams(vmem_limit_bytes=VMEM_BYTES),
        cost_estimate=pl.CostEstimate(flops=flops, bytes_accessed=moved, transcendentals=0),
        **extra,
    )


def shards(proj, cotangent, short_w, filter_in, filter_out, rates):
    sds = jax.ShapeDtypeStruct
    smem = pl.BlockSpec(memory_space=pltpu.SMEM)
    vmem = pl.BlockSpec(memory_space=pltpu.VMEM)
    channels, tokens = cotangent.shape
    devices = lax.axis_size("seq")
    groups = lax.axis_size("ch")
    length = devices * tokens
    rows = length // LANES
    lows = rows + 8
    features, order = filter_in.shape
    scale = 1.0 / math.sqrt(length)
    per = max(1, channels // devices)
    held = 4 * per
    step = max(8, held)
    start = lax.axis_index("seq") * per % channels

    tables = {name: jnp.asarray(value) for name, value in transform_tables(length).items()}
    first, last = tables["first"], tables["last"]
    middle, turn = tables["middle"], tables["turn"]

    packed = call(
        functools.partial(pack_kernel, per),
        sds((devices, held, tokens), BF16),
        in_specs=[vmem, vmem],
    )(proj, cotangent)
    recv = lax.all_to_all(packed, "seq", split_axis=0, concat_axis=0, tiled=True)

    own_short = lax.dynamic_slice_in_dim(short_w, start, per, 1).reshape(-1)
    own_rates = lax.dynamic_slice_in_dim(rates, start, per, 0)
    own_out = lax.dynamic_slice_in_dim(filter_out, start, per, 1)
    own_scale = 1.0 / jnp.sqrt(
        jnp.expm1(-2.0 * own_rates) / jnp.expm1(-2.0 * own_rates / length)
    )
    near, lane_table = feature_tables(length, features)
    block_rows = min(rows, 64)
    blocks = rows // block_rows
    block = block_rows * LANES
    near = near.reshape(2 * features, blocks, block_rows).transpose(1, 0, 2)
    in_high, in_low = split_outside(filter_in.T)
    out_high, out_low = split_outside(jnp.pad(own_out.T, ((0, 8 - per), (0, 0))))
    at_block = lambda height: pl.BlockSpec((height, block), lambda i: (0, i))
    fixed = lambda shape: pl.BlockSpec(shape, lambda i: (0,) * len(shape))
    near_block = pl.BlockSpec((1, 2 * features, block_rows), lambda i: (i, 0, 0))
    near, lane_table = jnp.asarray(near), jnp.asarray(lane_table)
    sine_high, sine_low, cosine, modulated = call(
        hidden_kernel,
        (
            sds((order, length), BF16),
            sds((order, length), BF16),
            sds((order, length), F32),
            sds((8, length), F32),
        ),
        grid=(blocks,),
        in_specs=[
            near_block,
            fixed((2 * features, LANES)),
            fixed((order, 3 * features)),
            fixed((8, 3 * order)),
        ],
        out_specs=(
            at_block(order),
            at_block(order),
            at_block(order),
            at_block(8),
        ),
        flops=8 * length * order * 3 * features,
        moved=length * order * 8,
    )(
        near,
        lane_table,
        jnp.concatenate([in_high, in_high, in_low], 1),
        jnp.concatenate([out_high, out_high, out_low], 1),
    )
    envelope, kernel_spec = call(
        functools.partial(filter_kernel, per, length),
        (sds((per * rows, LANES), F32), sds((per * lows, 2 * LANES), F32)),
        in_specs=[smem, smem] + [vmem] * 4,
        scratch=[pltpu.VMEM((rows * 8, LANES), F32)],
        flops=200 * length * LANES,
    )(own_rates, own_scale, modulated, first, middle, turn)

    raw, mixed, spec, weighted = call(
        functools.partial(spectra_kernel, per),
        (
            sds((rows * step, LANES), F32),
            sds((2 * per, rows, LANES), F32),
            sds((2 * per * lows, 2 * LANES), F32),
            sds((8, length), F32),
        ),
        in_specs=[smem] + [vmem] * 6,
        scratch=[pltpu.VMEM((rows * 8, LANES), F32)],
        flops=400 * length * LANES,
    )(own_short, recv, envelope, first, last, middle, turn)

    fo_high, fo_low = split_outside(jnp.pad(own_out, ((0, 0), (0, 8 - per))))
    out_grad, in_grad = call(
        filter_grad_kernel,
        (sds((8, order), F32), sds((features, order), F32)),
        grid=(blocks,),
        in_specs=[
            at_block(8),
            at_block(order),
            at_block(order),
            at_block(order),
            near_block,
            fixed((2 * features, LANES)),
            fixed((order, 24)),
        ],
        out_specs=(fixed((8, order)), fixed((features, order))),
        flops=200 * length * LANES,
    )(
        weighted,
        sine_high,
        sine_low,
        cosine,
        near,
        lane_table,
        jnp.concatenate([fo_high, fo_high, fo_low], 1),
    )

    others = [
        lax.ppermute(in_grad, "ch", [(i, (i + by) % groups) for i in range(groups)])
        for by in range(1, groups)
    ]
    slab_rows = max(16, held)
    slab = call(
        functools.partial(proj_grad_kernel, per, scale),
        sds((devices, slab_rows, tokens + 3 * LANES), BF16),
        in_specs=[smem] + [vmem] * 8,
        scratch=[pltpu.VMEM((rows * slab_rows, LANES), F32)],
        flops=400 * length * LANES,
    )(own_short, raw, mixed, spec, kernel_spec, out_grad, last, middle, turn)
    in_high, in_low = split_outside(functools.reduce(lambda a, b: a + b, others, in_grad) * scale)
    halves = jnp.concatenate([in_high, in_low], 1)
    halves = halves.reshape(2, features // 2, 2 * order).transpose(1, 0, 2)
    halves = halves.reshape(1, features // 2, 4 * order)
    halves = jnp.broadcast_to(halves, (devices,) + halves.shape[1:])
    slab = lax.dynamic_update_slice(slab, halves, (0, 0, tokens + LANES))

    back = lax.all_to_all(slab, "seq", split_axis=0, concat_axis=0, tiled=True)
    return call(
        functools.partial(unpack_kernel, per),
        (
            sds((3, channels, tokens), BF16),
            sds((3, channels, 3), F32),
            sds((order, channels), F32),
            sds((features, order), F32),
        ),
        in_specs=[vmem],
    )(back)


def solution(mesh):
    placed = (
        P(None, "ch", "seq"),
        P("ch", "seq"),
        P(None, "ch", None),
        P(),
        P(None, "ch"),
        P("ch"),
    )
    return jax.shard_map(
        shards,
        mesh=mesh,
        in_specs=placed,
        out_specs=(P(None, "ch", "seq"), P(None, "ch", None), P(None, "ch"), P()),
        check_vma=False,
    )
```

profile of v0, /device:TPU:0, one launch (start us, length us, event | category | flops | bytes accessed | tf_op | source)
XLA Modules:
  0.0 60.9 jit_solution(8579052298287880539)
XLA Ops:
  0.6 0.0 copy-start
  0.6 0.0 copy-start.3
  0.7 1.7 %shard_map.147 = bf16[8,16,1024]{2,1,0:T(8,128)(2,1)} custom-call(bf16[3,32,1024]{2,1,0:T(8,128)(2,1)} %proj_ref.1, bf16[32,1024]{1,0:T(8,128)(2,1)} %cot_ref.1), custom_call_target="tpu_custom_call" | custom-call | tf_op jit(solution)/shard_map/pallas_call | solution.py:450
  2.4 7.3 %all-to-all-start = ((bf16[8,16,1024]{2,1,0:T(8,128)(2,1)}), bf16[8,16,1024]{2,1,0:T(8,128)(2,1)S(1)}, u32[]{:S(2)}, u32[]{:S(2)}) async-start(bf16[8,16,1024]{2,1,0:T(8,128)(2,1)} %shard_map.147), calls=%async_computation | async-start | bytes 524288 | tf_op jit(solution)/shard_map/all_to_all | solution.py:455
  9.6 0.0 copy-done
  9.7 0.8 %copy.24 = f32[32,64]{0,1:T(8,128)S(1)} copy(f32[32,64]{1,0:T(8,128)} %param.15) | data formatting | bytes 16384 | tf_op args[3]
  10.5 0.8 %constant_dynamic-slice_fusion.1 = f32[3,4,3]{1,2,0:T(4,128)S(1)} fusion(f32[3,32,3]{1,2,0:T(4,128)} %param.14, s32[]{:T(128)S(6)} %select_n.13), kind=kLoop, calls=%fused_computation.20 | loop fusion | bytes 292 | tf_op jit(solution)/shard_map/dynamic_slice | solution.py:457
  11.2 0.1 copy.23
  11.4 0.6 %reshape.16.short_ref = f32[36]{0:T(128)} reshape(f32[3,4,3]{2,1,0:T(4,128)S(1)} %copy.23) | data formatting | bytes 288 | tf_op jit(solution)/shard_map/reshape | solution.py:457
  12.0 0.7 %copy.25.fo_ref = bf16[64,24]{1,0:T(8,128)(2,1)} copy(bf16[64,24]{0,1:T(8,128)(2,1)S(1)} %pad_maximum_fusion.2) | data formatting | bytes 6144 | tf_op jit(solution)/shard_map/concatenate | solution.py:547
  12.7 0.7 %pad_maximum_fusion.3.out_ref = bf16[8,192]{1,0:T(8,128)(2,1)} fusion(bf16[8,64]{1,0:T(8,128)(2,1)S(1)} %get-tuple-element.45, bf16[8,64]{1,0:T(8,128)(2,1)S(1)} %get-tuple-element.44), kind=kLoop, calls=%fused_computation.18 | loop fusion | flops 9216 | bytes 5120 | tf_op jit(solution)/shard_map/concatenate | solution.py:501
  13.4 0.7 %pad_maximum_fusion.in_ref = bf16[64,96]{1,0:T(8,128)(2,1)} fusion(bf16[64,32]{1,0:T(8,128)(2,1)S(1)} %get-tuple-element.41, bf16[64,32]{1,0:T(8,128)(2,1)S(1)} %get-tuple-element.40), kind=kLoop, calls=%fused_computation.7 | loop fusion | flops 36864 | bytes 20480 | tf_op jit(solution)/shard_map/concatenate | solution.py:500
  14.1 6.5 %shard_map.148 = (bf16[64,8192]{1,0:T(8,128)(2,1)}, bf16[64,8192]{1,0:T(8,128)(2,1)}, f32[64,8192]{1,0:T(8,128)}, f32[8,8192]{1,0:T(8,128)}) custom-call(f32[1,64,64]{2,1,0:T(8,128)} %constant.51.clone.near_ref, f32[64,128]{1,0:T(8,128)} %constant.52.clone.lane_ref, bf16[64,96]{1,0:T(8,128)(2,1)} %pad_maximum_fusion.in_ref, ...), custom_call_target="tpu_custom_call" | custom-call | flops 402653184 | bytes 4194304 | tf_op jit(solution)/shard_map/pallas_call | solution.py:474
  20.6 0.6 fusion.4
  21.2 2.3 %shard_map.149 = (f32[256,128]{1,0:T(8,128)}, f32[288,256]{1,0:T(8,128)}) custom-call(f32[4]{0:T(128)} %get-tuple-element.39.rates_ref, f32[4]{0:T(128)} %get-tuple-element.38.scale_ref, f32[8,8192]{1,0:T(8,128)} %get-tuple-element.16.mod_ref, bf16[144,192]{1,0:T(8,128)(2,1)} %constant.47.clone.first_ref, bf16[512,256]{1,0:T(8,128)(2,1)} %constant.49.clone.middle_ref, ...), custom_call_target="tpu_custom_call" | custom-call | flops 209715200 | tf_op jit(solution)/shard_map/pallas_call | solution.py:503
  23.5 0.0 all-to-all-done.recv_ref
  23.5 0.7 %copy-done.1 = bf16[8,16,1024]{2,1,0:T(8,128)(2,1)} copy-done((bf16[8,16,1024]{2,1,0:T(8,128)(2,1)}, bf16[8,16,1024]{2,1,0:T(8,128)(2,1)S(1)}, u32[]{:S(2)}) %copy-start.1) | copy-done | bytes 262168
  24.2 3.4 %shard_map.150 = (f32[1024,128]{1,0:T(8,128)}, f32[8,64,128]{2,1,0:T(8,128)}, f32[576,256]{1,0:T(8,128)}, f32[8,8192]{1,0:T(8,128)}) custom-call(f32[36]{0:T(128)} %reshape.16.short_ref, bf16[8,16,1024]{2,1,0:T(8,128)(2,1)} %copy-done.1, f32[256,128]{1,0:T(8,128)} %get-tuple-element.17.env_ref, bf16[144,192]{1,0:T(8,128)(2,1)} %constant.47.clone.first_ref, ...), custom_call_target="tpu_custom_call" | custom-call | flops 419430400 | tf_op jit(solution)/shard_map/pallas_call | solution.py:511
  27.5 4.5 %shard_map.151 = (f32[8,64]{1,0:T(8,128)}, f32[32,64]{1,0:T(8,128)}) custom-call(f32[8,8192]{1,0:T(8,128)} %get-tuple-element.22.weighted_ref, bf16[64,8192]{1,0:T(8,128)(2,1)} %get-tuple-element.23.sine_high_ref, bf16[64,8192]{1,0:T(8,128)(2,1)} %get-tuple-element.24.sine_low_ref, f32[64,8192]{1,0:T(8,128)} %get-tuple-element.25.cosine_ref, ...), custom_call_target="tpu_custom_call" | custom-call | flops 209715200 | tf_op jit(solution)/shard_map/pallas_call | solution.py:525
  32.1 0.0 collective-permute-start
  32.1 1.6 %collective-permute-start.1 = (f32[32,64]{1,0:T(8,128)}, f32[32,64]{1,0:T(8,128)S(1)}, u32[]{:S(2)}, u32[]{:S(2)}) collective-permute-start(f32[32,64]{1,0:T(8,128)} %get-tuple-element.27), channel_id=1, source_target_pairs={{0,2},{1,3},{2,0},{3,1},{4,6},{5,7},{6,4},{7,5},{8,10},{9,11},{10,... | collective-permute-start | bytes 24584 | tf_op jit(solution)/shard_map/ppermute | solution.py:551
  33.7 1.4 %collective-permute-start.2 = (f32[32,64]{1,0:T(8,128)}, f32[32,64]{1,0:T(8,128)S(1)}, u32[]{:S(2)}, u32[]{:S(2)}) collective-permute-start(f32[32,64]{1,0:T(8,128)} %get-tuple-element.27), channel_id=1, source_target_pairs={{0,3},{1,0},{2,1},{3,2},{4,7},{5,4},{6,5},{7,6},{8,11},{9,8},{10,9... | collective-permute-start | bytes 24584 | tf_op jit(solution)/shard_map/ppermute | solution.py:551
  35.1 3.5 %shard_map.152 = bf16[8,16,1408]{2,1,0:T(8,128)(2,1)} custom-call(f32[36]{0:T(128)} %reshape.16.short_ref, f32[1024,128]{1,0:T(8,128)} %get-tuple-element.18.raw_ref, f32[8,64,128]{2,1,0:T(8,128)} %get-tuple-element.19.mixed_ref, f32[576,256]{1,0:T(8,128)} %get-tuple-element.20.spec_ref, f32[288,256]{1,0:T(8,128)} %get-tuple-element.21.kernel_spec_ref, ...), custom_call_target="tpu_custom_call" | custom-call | flops 419430400 | tf_op jit(solution)/shard_map/pallas_call | solution.py:555
  38.5 0.0 collective-permute-done
  38.5 0.0 collective-permute-done.1
  38.5 0.0 collective-permute-done.2
  38.6 0.1 pad_maximum_fusion.1
  38.7 0.6 %broadcast_dynamic-update-slice_fusion = bf16[8,16,1408]{2,1,0:T(8,128)(2,1)} fusion(bf16[8,16,1408]{2,1,0:T(8,128)(2,1)} %shard_map.152, bf16[16,256]{1,0:T(8,128)(2,1)S(1)} %bitcast.13), kind=kLoop, calls=%fused_computation.3 | loop fusion | bytes 73728 | tf_op jit(solution)/shard_map/dynamic_update_slice | solution.py:567
  39.3 16.9 %all_to_all.10.recv_ref = bf16[8,16,1408]{2,1,0:T(8,128)(2,1)} all-to-all(bf16[8,16,1408]{2,1,0:T(8,128)(2,1)} %broadcast_dynamic-update-slice_fusion), channel_id=1, replica_groups=mesh['seq'=8,'ch'=4] {'seq'}, dimensions={0} | all-to-all | bytes 720896 | tf_op jit(solution)/shard_map/all_to_all | solution.py:569
  56.2 1.8 %shard_map.153 = (bf16[3,32,1024]{2,1,0:T(8,128)(2,1)}, f32[3,32,3]{2,1,0:T(8,128)}, f32[64,32]{1,0:T(8,128)}, f32[32,64]{1,0:T(8,128)}) custom-call(bf16[8,16,1408]{2,1,0:T(8,128)(2,1)} %all_to_all.10.recv_ref), custom_call_target="tpu_custom_call" | custom-call | tf_op jit(solution)/shard_map/pallas_call | solution.py:570
  58.0 1.4 %copy.28 = f32[64,32]{0,1:T(8,128)} copy(f32[64,32]{1,0:T(8,128)} %get-tuple-element.34) | data formatting | bytes 16384 | tf_op jit(solution)/shard_map/pallas_call | solution.py:570
  59.4 1.5 %copy.27 = f32[3,32,3]{1,2,0:T(4,128)} copy(f32[3,32,3]{2,1,0:T(8,128)} %get-tuple-element.33) | data formatting | bytes 2304 | tf_op jit(solution)/shard_map/pallas_call | solution.py:570
  (13 shorter events, 0.1 us)
Async XLA Ops:
  0.6 9.0 %copy-start = (f32[64,32]{0,1:T(8,128)S(1)}, f32[64,32]{0,1:T(8,128)}, u32[]{:S(2)}) copy-start(f32[64,32]{0,1:T(8,128)} %param.16) | copy-start | bytes 24580
  0.6 19.9 %copy-start.3 = (f32[32]{0:T(128)S(1)}, f32[32]{0:T(128)}, u32[]{:S(2)}) copy-start(f32[32]{0:T(128)} %param.17) | copy-start | bytes 388
  2.4 21.1 %all-to-all-start = ((bf16[8,16,1024]{2,1,0:T(8,128)(2,1)}), bf16[8,16,1024]{2,1,0:T(8,128)(2,1)S(1)}, u32[]{:S(2)}, u32[]{:S(2)}) async-start(bf16[8,16,1024]{2,1,0:T(8,128)(2,1)} %shard_map.147), calls=%async_computation | async-start | bytes 524288 | tf_op jit(solution)/shard_map/all_to_all | solution.py:455
  23.5 0.7 %copy-start.1 = (bf16[8,16,1024]{2,1,0:T(8,128)(2,1)}, bf16[8,16,1024]{2,1,0:T(8,128)(2,1)S(1)}, u32[]{:S(2)}) copy-start(bf16[8,16,1024]{2,1,0:T(8,128)(2,1)S(1)} %all-to-all-done.recv_ref) | copy-start | bytes 786436
  32.1 6.5 %copy-start.2 = (f32[32,64]{1,0:T(8,128)S(1)}, f32[32,64]{1,0:T(8,128)}, u32[]{:S(2)}) copy-start(f32[32,64]{1,0:T(8,128)} %get-tuple-element.27) | copy-start | bytes 24580
  32.1 6.5 %collective-permute-start = (f32[32,64]{1,0:T(8,128)}, f32[32,64]{1,0:T(8,128)S(1)}, u32[]{:S(2)}, u32[]{:S(2)}) collective-permute-start(f32[32,64]{1,0:T(8,128)} %get-tuple-element.27), channel_id=1, source_target_pairs={{0,1},{1,2},{2,3},{3,0},{4,5},{5,6},{6,7},{7,4},{8,9},{9,10},{10,1... | collective-permute-start | bytes 24584 | tf_op jit(solution)/shard_map/ppermute | solution.py:551
  32.1 6.5 %collective-permute-start.1 = (f32[32,64]{1,0:T(8,128)}, f32[32,64]{1,0:T(8,128)S(1)}, u32[]{:S(2)}, u32[]{:S(2)}) collective-permute-start(f32[32,64]{1,0:T(8,128)} %get-tuple-element.27), channel_id=1, source_target_pairs={{0,2},{1,3},{2,0},{3,1},{4,6},{5,7},{6,4},{7,5},{8,10},{9,11},{10,... | collective-permute-start | bytes 24584 | tf_op jit(solution)/shard_map/ppermute | solution.py:551
  33.7 4.9 %collective-permute-start.2 = (f32[32,64]{1,0:T(8,128)}, f32[32,64]{1,0:T(8,128)S(1)}, u32[]{:S(2)}, u32[]{:S(2)}) collective-permute-start(f32[32,64]{1,0:T(8,128)} %get-tuple-element.27), channel_id=1, source_target_pairs={{0,3},{1,0},{2,1},{3,2},{4,7},{5,4},{6,5},{7,6},{8,11},{9,8},{10,9... | collective-permute-start | bytes 24584 | tf_op jit(solution)/shard_map/ppermute | solution.py:551
where the time goes:
time: 61.6 us; the launch traced here: 60.9 us
  Pallas kernels  23.7 us (38%)
  blocking collectives  16.9 us (27%)
  starting transfers between devices  10.2 us (17%)
  local copies, waits for them, and re-layouts  7.3 us (12%)
  other arithmetic  2.09 us (3%)
  between operations  0.73 us (1%)
    all_to_all x1, blocking collectives, shards(): back = lax.all_to_all(slab, 'seq', split_axis=0, concat_axis=0, tiled=True)  16.9 us
    all_to_all x1, starting transfers between devices, shards(): lax.all_to_all(packed, 'seq', split_axis=0, concat_axis=0, tiled=True)  7.25 us
    pallas_call x1, Pallas kernels, shards(): call(hidden_kernel, (sds((order, length), BF16), sds((order, length), BF1...  6.48 us
    pallas_call x1, Pallas kernels, shards(): call(filter_grad_kernel, (sds((8, order), F32), sds((features, order), F3...  4.53 us
    pallas_call x1, Pallas kernels, shards(): call(functools.partial(proj_grad_kernel, per, scale), sds((devices, slab_...  3.47 us
    pallas_call x1, Pallas kernels, shards(): call(functools.partial(spectra_kernel, per), (sds((rows * step, LANES), F...  3.39 us
    ppermute x3, starting transfers between devices, shards(): lax.ppermute(in_grad, 'ch', [(i, (i + by) % groups) for i in range(groups)])  2.99 us
    pallas_call x2, local copies, waits for them, and re-layouts, shards(): call(functools.partial(unpack_kernel, per), (sds((3, channels, tokens), B...  2.91 us
  transfers between devices with their start and end apart: 4, of which 0 were waited for; matrix products, arithmetic and copies ran while one was open for 8% of the time, Pallas kernels for 20%

commit v1 on v0

v1 whole, which is shorter than its diff:
```python
import functools
import math

import jax
import jax.numpy as jnp
import ml_dtypes
import numpy as np
from jax import lax
from jax.experimental import pallas as pl
from jax.experimental.pallas import tpu as pltpu
from jax.sharding import PartitionSpec as P

F32 = jnp.float32
BF16 = jnp.bfloat16
LANES = 128
MIB = 1024 * 1024


def split(value):
    high = value.astype(BF16)
    return high, (value - high.astype(F32)).astype(BF16)


def np_split(value):
    high = value.astype(ml_dtypes.bfloat16)
    return high, (value - high.astype(np.float64)).astype(ml_dtypes.bfloat16)


def dot(left, right):
    return jnp.dot(left, right, preferred_element_type=F32)


def dot_first(left, right):
    return lax.dot_general(left, right, (((0,), (0,)), ((), ())), preferred_element_type=F32)


def dot_last(left, right):
    return lax.dot_general(left, right, (((1,), (1,)), ((), ())), preferred_element_type=F32)


@functools.lru_cache(maxsize=None)
def transform_tables(length):
    rows = length // LANES
    points = 2 * length
    lows = rows + 8
    low = np.arange(lows)
    row = np.arange(rows)
    lane = np.arange(LANES)
    angle = 2.0 * np.pi * ((low[:, None] * row[None, :]) % (2 * rows)) / (2 * rows)
    kept = (low <= rows)[:, None]
    first = np.concatenate([np.cos(angle) * kept, -np.sin(angle) * kept], 0)
    weight = np.where((low == 0) | (low == rows), 1.0, 2.0)[:, None] / points
    last = np.concatenate([np.cos(angle) * kept * weight, -np.sin(angle) * kept * weight], 0).T
    turn = 2.0 * np.pi * ((low[:, None] * lane[None, :]) % points) / points
    lane_angle = 2.0 * np.pi * ((lane[:, None] * lane[None, :]) % LANES) / LANES
    cosine, sine = np.cos(lane_angle), np.sin(lane_angle)
    middle = np.block([[cosine, -sine], [sine, cosine]])
    first_high, first_low = np_split(first)
    last_high, last_low = np_split(last)
    middle_high, middle_low = np_split(middle)
    return dict(
        first=np.concatenate([first_high, first_high, first_low], 1),
        last=np.concatenate([last_high, last_high, last_low], 1),
        middle=np.concatenate([middle_high, middle_low], 0),
        turn=np.concatenate([np.cos(turn), np.sin(turn)], 0).astype(np.float32),
    )


@functools.lru_cache(maxsize=None)
def feature_tables(length, feature_count):
    rows = length // LANES
    feature = np.arange(feature_count)
    multiplier = (1 + feature // 2 * 499) % length
    row_angle = 2.0 * np.pi * ((multiplier[:, None] * LANES * np.arange(rows)[None, :]) % length) / length
    lane_angle = 2.0 * np.pi * ((multiplier[:, None] * np.arange(LANES)[None, :]) % length) / length
    even = (feature % 2 == 0)[:, None]
    near = np.where(even, np.cos(row_angle), np.sin(row_angle))
    far = np.where(even, -np.sin(row_angle), np.cos(row_angle))
    return (
        np.concatenate([near, far], 0).astype(np.float32),
        np.concatenate([np.cos(lane_angle), np.sin(lane_angle)], 0).astype(np.float32),
    )


def middle_dot(value, middle_ref):
    high, low = split(value)
    size = 2 * LANES
    table_high, table_low = middle_ref[:size, :], middle_ref[size:, :]
    return dot(high, table_high) + dot(high, table_low) + dot(low, table_high)


def forward(signals, first_ref, middle_ref, turn_ref):
    lows = turn_ref.shape[0] // 2
    high, low = split(jnp.concatenate(signals, 1))
    partial = dot(first_ref[...], jnp.concatenate([high, low, high], 0))
    cosine, sine = turn_ref[:lows, :], turn_ref[lows:, :]
    turned = []
    for index in range(len(signals)):
        real = partial[:lows, index * LANES : (index + 1) * LANES]
        imag = partial[lows:, index * LANES : (index + 1) * LANES]
        turned.append(
            jnp.concatenate([real * cosine + imag * sine, imag * cosine - real * sine], 1)
        )
    return middle_dot(jnp.concatenate(turned, 0), middle_ref)


def backward(spectra, last_ref, middle_ref, turn_ref):
    lows = turn_ref.shape[0] // 2
    swapped = jnp.concatenate([jnp.concatenate([imag, real], 1) for real, imag in spectra], 0)
    partial = middle_dot(swapped, middle_ref)
    cosine, sine = turn_ref[:lows, :], turn_ref[lows:, :]
    turned = []
    for index in range(len(spectra)):
        imag = partial[index * lows : (index + 1) * lows, :LANES]
        real = partial[index * lows : (index + 1) * lows, LANES:]
        turned.append(
            jnp.concatenate([real * cosine - imag * sine, imag * cosine + real * sine], 0)
        )
    high, low = split(jnp.concatenate(turned, 1))
    result = dot(last_ref[...], jnp.concatenate([high, low, high], 0))
    return [result[:, index * LANES : (index + 1) * LANES] for index in range(len(spectra))]


def later(value):
    turned = pltpu.roll(value, 1, 1)
    carried = pltpu.roll(turned, 1, 0)
    row = lax.broadcasted_iota(jnp.int32, value.shape, 0)
    lane = lax.broadcasted_iota(jnp.int32, value.shape, 1)
    carried = jnp.where(row == 0, 0.0, carried)
    return jnp.where(lane == 0, carried, turned)


def sooner(value):
    rows = value.shape[0]
    turned = pltpu.roll(value, LANES - 1, 1)
    carried = pltpu.roll(turned, rows - 1, 0)
    row = lax.broadcasted_iota(jnp.int32, value.shape, 0)
    lane = lax.broadcasted_iota(jnp.int32, value.shape, 1)
    carried = jnp.where(row == rows - 1, 0.0, carried)
    return jnp.where(lane == LANES - 1, carried, turned)


def sine_cosine(half_angle):
    turns = jnp.round(half_angle * (1.0 / math.pi))
    rest = half_angle - turns * 3.140625
    rest = rest - turns * 9.67653589793e-4
    square = rest * rest
    sine = 2.59045638e-06
    for coefficient in (-1.98008819e-04, 8.33289957e-03, -1.66666476e-01, 9.99999977e-01):
        sine = sine * square + coefficient
    cosine = 2.31536124e-05
    for coefficient in (-1.38536905e-03, 4.16635829e-02, -4.99999053e-01, 9.99999953e-01):
        cosine = cosine * square + coefficient
    sine = sine * rest
    twice = sine + sine
    return twice * cosine, 1.0 - twice * sine


def first_channel(per, channels):
    return lax.axis_index("seq") * per % channels


def own_rows(per, out_ref):
    channels = out_ref.shape[0]
    start = first_channel(per, channels)
    return pltpu.roll(out_ref[...], lax.rem(channels - start, channels), 0)[:8, :]


def tap_rows(short_ref):
    return jnp.concatenate([short_ref[index] for index in range(3)], 0)


def own_columns(per, value):
    channels = value.shape[1]
    start = first_channel(per, channels)
    turned = pltpu.roll(value, lax.rem(channels - start, channels), 1)
    return [turned[:, channel : channel + 1] for channel in range(per)]


def small_expm1(value):
    total = 1.0
    for divisor in (7.0, 6.0, 5.0, 4.0, 3.0, 2.0):
        total = 1.0 + total * value * (1.0 / divisor)
    return total * value


def pack_kernel(per, proj_ref, cot_ref, out_ref):
    channels = cot_ref.shape[0]
    whole = [proj_ref[index].astype(F32) for index in range(3)] + [cot_ref[...].astype(F32)]
    for device in range(out_ref.shape[0]):
        start = device * per % channels
        rows = jnp.concatenate([part[start : start + per, :] for part in whole], 0)
        out_ref[device] = rows.astype(BF16)


def block_features(table, lane_ref):
    count = lane_ref.shape[0] // 2
    lane_cos, lane_sin = lane_ref[:count, :], lane_ref[count:, :]
    near, far = table[:count, :], table[count:, :]
    rows = range(table.shape[1])
    blocks = [near[:, row : row + 1] * lane_cos + far[:, row : row + 1] * lane_sin for row in rows]
    return split(jnp.concatenate(blocks, 1))


def in_blocks(blocks, body):
    if blocks == 1:
        body(0)
    else:
        lax.fori_loop(0, blocks, lambda index, carry: (body(index), carry)[1], 0)


def block_copies(index, block, here, there, semaphores, outward):
    columns = pl.ds(pl.multiple_of(index * block, LANES), block)
    pairs = [(near, far.at[:, columns]) for near, far in zip(here, there, strict=True)]
    return [
        pltpu.make_async_copy(*(pair if outward else pair[::-1]), semaphores.at[at])
        for at, pair in enumerate(pairs)
    ]


def filter_kernel(per, length, blocks, *refs):
    given, loaded = refs[:10], refs[10:20]
    env_ref, spec_ref = refs[20:22]
    hidden_refs, buffers = refs[22:25], refs[25:28]
    mod_ref, stage_ref, load_semaphores, out_semaphores = refs[28:]
    loads = [
        pltpu.make_async_copy(source, target, load_semaphores.at[index])
        for index, (source, target) in enumerate(zip(given, loaded, strict=True))
    ]
    for load in loads:
        load.start()
    for load in loads:
        load.wait()
    first_ref, _, middle_ref, turn_ref, near_ref, lane_ref, in_ref, out_ref, rates_ref, _ = loaded
    rows = length // LANES
    block = length // blocks
    block_rows = rows // blocks
    sine_high_ref, sine_low_ref, cosine_ref = buffers
    in_high, in_low = split(in_ref[...] * 0.5)
    in_weights = jnp.concatenate([in_high, in_high, in_low], 0)
    out_high, out_low = split(own_rows(per, out_ref))
    out_weights = jnp.concatenate([out_high, out_high, out_low], 1)

    def hidden_block(index):
        high, low = block_features(near_ref[index], lane_ref)
        half_angle = dot_first(in_weights, jnp.concatenate([high, low, high], 0))
        sine, cosine = sine_cosine(half_angle)
        cosine_ref[...] = cosine
        high, low = split(sine)
        sine_high_ref[...] = high
        sine_low_ref[...] = low
        copies = block_copies(index, block, buffers, hidden_refs, out_semaphores, True)
        for copy in copies:
            copy.start()
        mod_ref[...] = dot(out_weights, jnp.concatenate([high, low, high], 0))
        for row in range(block_rows):
            at = pl.multiple_of((index * block_rows + row) * 8, 8)
            stage_ref[pl.ds(at, 8), :] = mod_ref[:, row * LANES : (row + 1) * LANES]
        if blocks > 1:
            for copy in copies:
                copy.wait()

    in_blocks(blocks, hidden_block)
    rates = own_columns(per, rates_ref[...])
    position = lax.broadcasted_iota(jnp.int32, (rows, LANES), 0) * LANES
    position = position + lax.broadcasted_iota(jnp.int32, (rows, LANES), 1)
    relative = position.astype(F32) * (1.0 / length)
    kernels = []
    for channel in range(per):
        rate = -2.0 * jnp.broadcast_to(rates[channel], (8, LANES))
        inverse = jnp.sqrt(small_expm1(rate * (1.0 / length)) / (jnp.exp(rate) - 1.0))
        envelope = jnp.exp(0.5 * rate[:1, :] * relative) * inverse[:1, :]
        env_ref[channel * rows : (channel + 1) * rows, :] = envelope
        kernels.append(envelope * stage_ref[pl.ds(channel, rows, stride=8), :])
    spec_ref[...] = forward(kernels, first_ref, middle_ref, turn_ref)
    if blocks == 1:
        for copy in block_copies(0, block, buffers, hidden_refs, out_semaphores, True):
            copy.wait()


def signal_kernel(per, blocks, *refs):
    recv_ref, env_ref, first_ref, last_ref, middle_ref, turn_ref = refs[:6]
    near_ref, lane_ref, out_ref, short_ref = refs[6:10]
    hidden_refs = refs[10:13]
    raw_ref, mixed_ref, spec_ref, out_grad_ref, in_grad_ref = refs[13:18]
    buffers = refs[18:21]
    stage_ref, weighted_ref, semaphores = refs[21:]
    devices, held, tokens = recv_ref.shape
    rows = devices * tokens // LANES
    block = rows * LANES // blocks
    block_rows = rows // blocks
    step = raw_ref.shape[0] // rows
    lows = turn_ref.shape[0] // 2
    for copy in block_copies(0, block, buffers, hidden_refs, semaphores, False):
        copy.start()
    taps = own_columns(per, tap_rows(short_ref))
    for device in range(devices):
        for part in range(tokens // LANES):
            at = (device * (tokens // LANES) + part) * step
            raw_ref[at : at + held, :] = recv_ref[
                device, :, part * LANES : (part + 1) * LANES
            ].astype(F32)
    gated, grads = [], []
    for channel in range(per):
        mixed = []
        for index in range(3):
            base = raw_ref[pl.ds(index * per + channel, rows, stride=step), :]
            total = taps[channel][3 * index : 3 * index + 1, :] * base
            for tap in (1, 2):
                base = later(base)
                total = total + taps[channel][3 * index + tap : 3 * index + tap + 1, :] * base
            mixed.append(total)
        cotangent = raw_ref[pl.ds(3 * per + channel, rows, stride=step), :]
        mixed_ref[2 * channel] = mixed[1]
        mixed_ref[2 * channel + 1] = mixed[2]
        gated.append(mixed[1] * mixed[2])
        grads.append(cotangent * mixed[0])
    spectra = forward(gated + grads, first_ref, middle_ref, turn_ref)
    spec_ref[...] = spectra
    products = []
    for channel in range(per):
        at, other = channel * lows, (per + channel) * lows
        gated_real, gated_imag = spectra[at : at + lows, :LANES], spectra[at : at + lows, LANES:]
        grad_real, grad_imag = (
            spectra[other : other + lows, :LANES],
            spectra[other : other + lows, LANES:],
        )
        products.append(
            (
                grad_real * gated_real + grad_imag * gated_imag,
                grad_imag * gated_real - grad_real * gated_imag,
            )
        )
    results = backward(products, last_ref, middle_ref, turn_ref)
    if per < 8:
        stage_ref[...] = jnp.zeros_like(stage_ref)
    for channel in range(per):
        weighted = results[channel] * env_ref[channel * rows : (channel + 1) * rows, :]
        stage_ref[pl.ds(channel, rows, stride=8), :] = weighted
    out_rows = own_rows(per, out_ref)
    out_rounded = out_rows.astype(BF16).astype(F32)
    weights = jnp.concatenate([out_rows, out_rows, out_rows - out_rounded], 0).astype(BF16)
    out_grad_ref[...] = jnp.zeros_like(out_grad_ref)
    in_grad_ref[...] = jnp.zeros_like(in_grad_ref)

    def add_block(index):
        copies = block_copies(index, block, buffers, hidden_refs, semaphores, False)
        if blocks > 1:

            @pl.when(index > 0)
            def _():
                for copy in copies:
                    copy.start()

        for row in range(block_rows):
            at = pl.multiple_of((index * block_rows + row) * 8, 8)
            weighted_ref[:, row * LANES : (row + 1) * LANES] = stage_ref[pl.ds(at, 8), :]
        count = lane_ref.shape[0] // 2
        feature_high, feature_low = block_features(near_ref[index], lane_ref)
        weighted = weighted_ref[...]
        high = weighted.astype(BF16)
        rounded = high.astype(F32)
        both = jnp.concatenate([weighted, weighted - rounded], 0).astype(BF16)
        terms = jnp.concatenate([weighted, weighted - rounded, weighted], 0).astype(BF16)
        grad = dot_first(weights, terms)
        for copy in copies:
            copy.wait()
        sine_high_ref, sine_low_ref, cosine_ref = buffers
        total = dot_last(both, sine_high_ref[...])
        out_grad_ref[...] += total[:8] + total[8:] + dot_last(high, sine_low_ref[...])
        grad_high, grad_low = split(grad * cosine_ref[...])
        total = dot_last(jnp.concatenate([feature_high, feature_low], 0), grad_high)
        in_grad_ref[...] += total[:count] + total[count:] + dot_last(feature_high, grad_low)

    in_blocks(blocks, add_block)


def proj_grad_kernel(
    per,
    scale,
    short_ref,
    raw_ref,
    mixed_ref,
    spec_ref,
    kernel_spec_ref,
    out_grad_ref,
    last_ref,
    middle_ref,
    turn_ref,
    slab_ref,
    stage_ref,
):
    devices, held, width = slab_ref.shape
    tokens = width - LANES
    rows = devices * tokens // LANES
    taps = own_columns(per, tap_rows(short_ref))
    step = raw_ref.shape[0] // rows
    lows = turn_ref.shape[0] // 2
    products = []
    for sign in (1.0, -1.0):
        for channel in range(per):
            at = (channel if sign > 0 else per + channel) * lows
            real, imag = spec_ref[at : at + lows, :LANES], spec_ref[at : at + lows, LANES:]
            at = channel * lows
            kernel_real = kernel_spec_ref[at : at + lows, :LANES]
            kernel_imag = sign * kernel_spec_ref[at : at + lows, LANES:]
            products.append(
                (
                    real * kernel_real - imag * kernel_imag,
                    real * kernel_imag + imag * kernel_real,
                )
            )
    results = backward(products, last_ref, middle_ref, turn_ref)
    sums = [None] * (3 * per)
    for channel in range(per):
        cotangent = raw_ref[pl.ds(3 * per + channel, rows, stride=step), :]
        grad_mixed = (
            cotangent * results[channel],
            results[per + channel] * mixed_ref[2 * channel + 1],
            results[per + channel] * mixed_ref[2 * channel],
        )
        for index in range(3):
            base = raw_ref[pl.ds(index * per + channel, rows, stride=step), :]
            grad = grad_mixed[index]
            total = taps[channel][3 * index : 3 * index + 1, :] * grad
            parts = [jnp.sum(grad * base, axis=0, keepdims=True)]
            moved = grad
            for tap in (1, 2):
                base = later(base)
                moved = sooner(moved)
                total = total + taps[channel][3 * index + tap : 3 * index + tap + 1, :] * moved
                parts.append(jnp.sum(grad * base, axis=0, keepdims=True))
            sums[index * per + channel] = jnp.concatenate(parts, 0)
            stage_ref[pl.ds(index * per + channel, rows, stride=held), :] = total
    for device in range(devices):
        for part in range(tokens // LANES):
            at = (device * (tokens // LANES) + part) * held
            slab_ref[device, :, part * LANES : (part + 1) * LANES] = stage_ref[
                at : at + held, :
            ].astype(BF16)
    row = lax.broadcasted_iota(jnp.int32, (held, LANES), 0)
    lane = lax.broadcasted_iota(jnp.int32, (held, LANES), 1)
    small = jnp.zeros((held, LANES), F32)
    for place in range(3 * per):
        total = jnp.sum(sums[place], axis=1, keepdims=True) * scale
        for tap in range(3):
            small = jnp.where((row == 4 + place) & (lane == tap), total[tap : tap + 1, :], small)
    order = out_grad_ref.shape[1]
    out_grad = jnp.concatenate(
        [out_grad_ref[...] * scale, jnp.zeros((8, LANES - order), F32)], 1
    )
    out_grad = jnp.concatenate([out_grad, jnp.zeros((held - 8, LANES), F32)], 0)
    small = jnp.where(row < per, out_grad, small)
    rest = pltpu.roll(small - small.astype(BF16).astype(F32), LANES // 2, 1)
    small = jnp.where(lane < LANES // 2, small, rest).astype(BF16)
    for device in range(devices):
        slab_ref[device, :, tokens:] = small


def finish_kernel(scale, slab_ref, *refs):
    parts, result_ref = refs[:-1], refs[-1]
    total = parts[0][...]
    for part in parts[1:]:
        total = total + part[...]
    total = total * scale
    rounded = total.astype(BF16).astype(F32)
    halves = jnp.concatenate([total, total - rounded], 1)
    held = slab_ref.shape[1]
    count = halves.shape[0] // 4
    wide = jnp.concatenate([halves[4 * index : 4 * index + 4, :] for index in range(count)], 1)
    wide = jnp.concatenate([jnp.zeros((held - 4, wide.shape[1]), F32), wide], 0)
    keep = lax.broadcasted_iota(jnp.int32, wide.shape, 0) < held - 4
    for device in range(slab_ref.shape[0]):
        main = slab_ref[device, :, : wide.shape[1]].astype(F32)
        result_ref[device, :, : wide.shape[1]] = jnp.where(keep, main, wide).astype(BF16)
        result_ref[device, :, wide.shape[1] :] = slab_ref[device, :, wide.shape[1] :]


def unpack_kernel(per, recv_ref, proj_ref, short_ref, out_ref, in_ref):
    channels, tokens = proj_ref.shape[1:]
    devices = channels // per
    held = recv_ref.shape[1]
    features, order = in_ref.shape
    for index in range(3):
        rows = [
            recv_ref[device, index * per : (index + 1) * per, :tokens].astype(F32)
            for device in range(devices)
        ]
        proj_ref[index] = jnp.concatenate(rows, 0).astype(BF16)
    small = [recv_ref[device, :, tokens:].astype(F32) for device in range(devices)]
    small = [part + pltpu.roll(part, LANES // 2, 1) for part in small]
    for index in range(3):
        at = 4 + index * per
        rows = jnp.concatenate([part[at : at + per, :] for part in small], 0)
        short_ref[index] = rows.T[:3, :]
    out_ref[...] = jnp.concatenate([part[:per, :order] for part in small], 0)
    count = features // 4
    total = recv_ref[0, held - 4 :, : count * LANES].astype(F32)
    for device in range(1, devices):
        total = total + recv_ref[device, held - 4 :, : count * LANES].astype(F32)
    total = jnp.concatenate(
        [total[:, index * LANES : (index + 1) * LANES] for index in range(count)], 0
    )
    in_ref[...] = total[:, :order] + total[:, order:]


def call(kernel, out, limit, in_specs=None, out_specs=None, flops=0, moved=0, **more):
    vmem = pl.BlockSpec(memory_space=pltpu.VMEM)
    return pl.pallas_call(
        kernel,
        out_shape=out,
        in_specs=in_specs,
        out_specs=out_specs if out_specs is not None else jax.tree.map(lambda _: vmem, out),
        compiler_params=pltpu.CompilerParams(vmem_limit_bytes=limit),
        cost_estimate=pl.CostEstimate(flops=flops, bytes_accessed=moved, transcendentals=0),
        **more,
    )


def shards(proj, cotangent, short_w, filter_in, filter_out, rates):
    vmem = pl.BlockSpec(memory_space=pltpu.VMEM)
    hbm = pl.BlockSpec(memory_space=pltpu.HBM)
    channels, tokens = cotangent.shape
    devices = lax.axis_size("seq")
    groups = lax.axis_size("ch")
    length = devices * tokens
    rows = length // LANES
    lows = rows + 8
    features, order = filter_in.shape
    scale = 1.0 / math.sqrt(length)
    per = max(1, channels // devices)
    held = 4 * per
    step = max(8, held)
    small = length * order * 8 <= 8 * MIB
    limit = (24 if small else 56) * MIB
    sds = jax.ShapeDtypeStruct
    made = pltpu.VMEM if small else sds
    put = (lambda x: pltpu.with_memory_space_constraint(x, pltpu.VMEM)) if small else (lambda x: x)
    keep = lambda x: pltpu.with_memory_space_constraint(x, pltpu.HBM)

    packed = call(
        functools.partial(pack_kernel, per),
        made((devices, held, tokens), BF16),
        limit,
        in_specs=[vmem, vmem],
    )(keep(proj), keep(cotangent))
    recv = lax.all_to_all(packed, "seq", split_axis=0, concat_axis=0, tiled=True)

    near, lane_table = feature_tables(length, features)
    blocks = max(1, rows // 64)
    block = length // blocks
    near = near.reshape(2 * features, blocks, rows // blocks).transpose(1, 0, 2)
    tables = transform_tables(length)
    given = [tables[name] for name in ("first", "last", "middle", "turn")] + [near, lane_table]
    given = [jnp.asarray(value) for value in given]
    given += [filter_in, filter_out.T, rates.reshape(1, channels), short_w.transpose(0, 2, 1)]
    hidden = tuple(pltpu.HBM((order, length), kind) for kind in (BF16, BF16, F32))
    buffers = [pltpu.VMEM((order, block), kind) for kind in (BF16, BF16, F32)]
    *loaded, envelope, kernel_spec, sine_high, sine_low, cosine = call(
        functools.partial(filter_kernel, per, length, blocks),
        tuple(made(value.shape, value.dtype) for value in given)
        + (made((per * rows, LANES), F32), made((per * lows, 2 * LANES), F32))
        + hidden,
        limit,
        in_specs=[hbm] * len(given),
        out_specs=(vmem,) * (len(given) + 2) + (hbm,) * 3,
        scratch_shapes=buffers
        + [
            pltpu.VMEM((8, block), F32),
            pltpu.VMEM((rows * 8, LANES), F32),
            pltpu.SemaphoreType.DMA((len(given),)),
            pltpu.SemaphoreType.DMA((3,)),
        ],
        flops=8 * length * order * 3 * features,
        moved=length * order * 8,
    )(*[keep(value) for value in given])
    first, last, middle, turn, near, lane_table, _, out_rows, _, short_taps = map(put, loaded)

    raw, mixed, spec, out_grad, in_grad = call(
        functools.partial(signal_kernel, per, blocks),
        (
            made((rows * step, LANES), F32),
            made((2 * per, rows, LANES), F32),
            made((2 * per * lows, 2 * LANES), F32),
            made((8, order), F32),
            sds((features, order), F32),
        ),
        limit,
        in_specs=[vmem] * 10 + [hbm] * 3,
        scratch_shapes=buffers
        + [
            pltpu.VMEM((rows * 8, LANES), F32),
            pltpu.VMEM((8, block), F32),
            pltpu.SemaphoreType.DMA((3,)),
        ],
        flops=400 * length * LANES,
    )(
        put(recv),
        put(envelope),
        first,
        last,
        middle,
        turn,
        near,
        lane_table,
        out_rows,
        short_taps,
        keep(sine_high),
        keep(sine_low),
        keep(cosine),
    )

    others = [
        lax.ppermute(in_grad, "ch", [(i, (i + by) % groups) for i in range(groups)])
        for by in range(1, groups)
    ]
    slab_rows = max(16, held)
    slab = call(
        functools.partial(proj_grad_kernel, per, scale),
        made((devices, slab_rows, tokens + LANES), BF16),
        limit,
        in_specs=[vmem] + [vmem] * 8,
        scratch_shapes=[pltpu.VMEM((rows * slab_rows, LANES), F32)],
        flops=400 * length * LANES,
    )(short_taps, put(raw), put(mixed), put(spec), put(kernel_spec), put(out_grad), last, middle, turn)
    slab = call(
        functools.partial(finish_kernel, scale),
        sds((devices, slab_rows, tokens + LANES), BF16),
        limit,
        in_specs=[vmem] * (groups + 1),
    )(put(slab), in_grad, *others)

    back = lax.all_to_all(slab, "seq", split_axis=0, concat_axis=0, tiled=True)
    grad_proj, grad_short, grad_out, grad_in = call(
        functools.partial(unpack_kernel, per),
        (
            sds((3, channels, tokens), BF16),
            sds((3, 3, channels), F32),
            sds((channels, order), F32),
            sds((features, order), F32),
        ),
        limit,
        in_specs=[vmem],
    )(back)
    return grad_proj, grad_short.transpose(0, 2, 1), grad_out.T, grad_in


def solution(mesh):
    placed = (
        P(None, "ch", "seq"),
        P("ch", "seq"),
        P(None, "ch", None),
        P(),
        P(None, "ch"),
        P("ch"),
    )
    return jax.shard_map(
        shards,
        mesh=mesh,
        in_specs=placed,
        out_specs=(P(None, "ch", "seq"), P(None, "ch", None), P(None, "ch"), P()),
        check_vma=False,
    )
```

time: 61.6 us -> 42.4 us (0.69)
  Pallas kernels: 23.7 us -> 15.3 us
  local copies, waits for them, and re-layouts: 7.3 us -> 0 us
  waiting for transfers between devices: 0.01 us -> 3.96 us
  blocking collectives: 16.9 us -> 13.2 us
  other arithmetic: 2.09 us -> 0 us
  starting transfers between devices: 10.2 us -> 9.06 us
    pallas_call x6 -> x5, Pallas kernels: 21.9 us -> 14.4 us  [the longest x1 6.68 us: shards(): call(functools.partial(filter_kernel, per, length, blocks), tuple((made(v...]
    all_to_all x1, blocking collectives: 16.9 us -> 13.2 us  [shards(): back = lax.all_to_all(slab, 'seq', split_axis=0, concat_axis=0, tiled=True)]
    pallas_call x2 -> x0, local copies, waits for them, and re-layouts: 2.91 us -> none  [shards(): call(functools.partial(unpack_kernel, per), (sds((3, channels, tokens), B...]
    all_to_all x1, waiting for transfers between devices: 0.01 us -> 2.23 us  [shards(): lax.all_to_all(packed, 'seq', split_axis=0, concat_axis=0, tiled=True)]
    ppermute x3, waiting for transfers between devices: 0.01 us -> 1.73 us  [shards(): lax.ppermute(in_grad, 'ch', [(i, (i + by) % groups) for i in range(groups)])]
    unnamed x9 -> x0, local copies, waits for them, and re-layouts: 1.51 us -> none
    concatenate x4 -> x0, other arithmetic: 1.45 us -> none  [the longest x1 0.69 us: shards(): jnp.concatenate([in_high, in_high, in_low], 1)]
    ppermute x3, starting transfers between devices: 2.99 us -> 1.81 us  [shards(): lax.ppermute(in_grad, 'ch', [(i, (i + by) % groups) for i in range(groups)])]
  transfers between devices with their start and end apart: 4 -> 4, of which waited for: 0 -> 3; matrix products, arithmetic and copies ran while one was open for 8% -> 0% of each run, Pallas kernels for 20% -> 19%
where the time goes in v1:
time: 42.4 us; the launch traced here: 42.1 us
  Pallas kernels  15.3 us (36%)
  blocking collectives  13.2 us (31%)
  starting transfers between devices  9.06 us (21%)
  waiting for transfers between devices  3.96 us (9%)
  between operations  0.68 us (2%)
    all_to_all x1, blocking collectives, shards(): back = lax.all_to_all(slab, 'seq', split_axis=0, concat_axis=0, tiled=True)  13.2 us
    all_to_all x1, starting transfers between devices, shards(): lax.all_to_all(packed, 'seq', split_axis=0, concat_axis=0, tiled=True)  7.25 us
    pallas_call x1, Pallas kernels, shards(): call(functools.partial(filter_kernel, per, length, blocks), tuple((made(v...  6.68 us
    pallas_call x1, Pallas kernels, shards(): call(functools.partial(signal_kernel, per, blocks), (made((rows * step, L...  4.7 us
    all_to_all x1, waiting for transfers between devices, shards(): lax.all_to_all(packed, 'seq', split_axis=0, concat_axis=0, tiled=True)  2.23 us
    ppermute x3, starting transfers between devices, shards(): lax.ppermute(in_grad, 'ch', [(i, (i + by) % groups) for i in range(groups)])  1.81 us
    ppermute x3, waiting for transfers between devices, shards(): lax.ppermute(in_grad, 'ch', [(i, (i + by) % groups) for i in range(groups)])  1.73 us
    pallas_call x1, Pallas kernels, shards(): call(functools.partial(pack_kernel, per), made((devices, held, tokens), B...  1.7 us
  transfers between devices with their start and end apart: 4, of which 3 were waited for; matrix products, arithmetic and copies ran while one was open for 0% of the time, Pallas kernels for 19%

profile of v1, /device:TPU:0, one launch (start us, length us, event | category | flops | bytes accessed | tf_op | source)
XLA Modules:
  0.0 42.1 jit_solution(9120400811508393900)
XLA Ops:
  0.6 1.7 %shard_map.148 = bf16[8,16,1024]{2,1,0:T(8,128)(2,1)} custom-call(bf16[3,32,1024]{2,1,0:T(8,128)(2,1)} %proj_ref.1, bf16[32,1024]{1,0:T(8,128)(2,1)} %cot_ref.1), custom_call_target="tpu_custom_call" | custom-call | tf_op jit(solution)/shard_map/pallas_call | solution.py:541
  2.3 7.3 %all-to-all-start = ((bf16[8,16,1024]{2,1,0:T(8,128)(2,1)}), bf16[8,16,1024]{2,1,0:T(8,128)(2,1)S(1)}, u32[]{:S(2)}, u32[]{:S(2)}) async-start(bf16[8,16,1024]{2,1,0:T(8,128)(2,1)} %shard_map.148), calls=%async_computation | async-start | bytes 524288 | tf_op jit(solution)/shard_map/all_to_all | solution.py:547
  9.6 6.7 %shard_map.147 = (bf16[144,192]{1,0:T(8,128)(2,1)S(1)}, bf16[64,432]{1,0:T(8,128)(2,1)S(1)}, bf16[512,256]{1,0:T(8,128)(2,1)S(1)}, f32[144,128]{1,0:T(8,128)S(1)...) custom-call(bf16[144,192]{1,0:T(8,128)(2,1)} %constant.12.clone.refs, ...), custom_call_target="tpu_custom_call" | custom-call | flops 402653184 | bytes 4194304 | tf_op jit(solution)/shard_map/pallas_call | solution.py:559
  16.3 2.2 %all-to-all-done.refs_0_ = bf16[8,16,1024]{2,1,0:T(8,128)(2,1)S(1)} async-done(((bf16[8,16,1024]{2,1,0:T(8,128)(2,1)}), bf16[8,16,1024]{2,1,0:T(8,128)(2,1)S(1)}, u32[]{:S(2)}, u32[]{:S(2)}) %all-to-all-start) | async-done | bytes 262176 | tf_op jit(solution)/shard_map/all_to_all | solution.py:547
  18.5 4.7 %shard_map.149 = (f32[1024,128]{1,0:T(8,128)S(1)}, f32[8,64,128]{2,1,0:T(8,128)S(1)}, f32[576,256]{1,0:T(8,128)S(1)}, f32[8,64]{1,0:T(8,128)S(1)}, f32[32,64]{1,0:T(8,128)S(1)}) custom-call(bf16[8,16,1024]{2,1,0:T(8,128)(2,1)S(1)} %all-to-all-done.refs_0_, f32[256,128]{1,0:T(8,128)S(1)} %get-tuple-element.27.refs_1_, ...), custom_call_target="tpu_custom_call" | custom-call | flops 419430400 | tf_op jit(solution)/shard_map/pallas_call | solution.py:579
  23.2 0.1 collective-permute-start.2
  23.3 1.6 %collective-permute-start.1 = (f32[32,64]{1,0:T(8,128)S(1)}, f32[32,64]{1,0:T(8,128)S(1)}, u32[]{:S(2)}, u32[]{:S(2)}) collective-permute-start(f32[32,64]{1,0:T(8,128)S(1)} %get-tuple-element.43.refs_0_), channel_id=1, source_target_pairs={{0,2},{1,3},{2,0},{3,1},{4,6},{5,7},{6,4},{7,5},{8,10},{9,11},{10,... | collective-permute-start | bytes 24584 | tf_op jit(solution)/shard_map/ppermute | solution.py:614
  24.9 0.2 collective-permute-start
  25.0 1.3 %shard_map.150.slab_ref = bf16[8,16,1152]{2,1,0:T(8,128)(2,1)S(1)} custom-call(f32[3,3,32]{2,1,0:T(4,128)S(1)} %get-tuple-element.26.refs_9_.short_ref, f32[1024,128]{1,0:T(8,128)S(1)} %get-tuple-element.38.raw_ref, f32[8,64,128]{2,1,0:T(8,128)S(1)} %get-tuple-element.39.mixed_ref, f32[576,256]{1,0:T(8,128)S(1)} %get-tuple-element.40.spec_ref, ...), custom_call_target="tpu_custom_call" | custom-call | flops 419430400 | tf_op jit(solution)/shard_map/pallas_call | solution.py:618
  26.3 0.0 collective-permute-done.2.refs_3_
  26.3 0.8 %collective-permute-done.1.refs_2_ = f32[32,64]{1,0:T(8,128)S(1)} collective-permute-done((f32[32,64]{1,0:T(8,128)S(1)}, f32[32,64]{1,0:T(8,128)S(1)}, u32[]{:S(2)}, u32[]{:S(2)}) %collective-permute-start.1) | collective-permute-done | bytes 8224 | tf_op jit(solution)/shard_map/ppermute | solution.py:614
  27.1 0.9 %collective-permute-done.refs_1_ = f32[32,64]{1,0:T(8,128)S(1)} collective-permute-done((f32[32,64]{1,0:T(8,128)S(1)}, f32[32,64]{1,0:T(8,128)S(1)}, u32[]{:S(2)}, u32[]{:S(2)}) %collective-permute-start) | collective-permute-done | bytes 8224 | tf_op jit(solution)/shard_map/ppermute | solution.py:614
  28.0 0.1 shard_map.151
  28.1 13.2 %all_to_all.10.recv_ref = bf16[8,16,1152]{2,1,0:T(8,128)(2,1)S(1)} all-to-all(bf16[8,16,1152]{2,1,0:T(8,128)(2,1)S(1)} %shard_map.151), channel_id=1, replica_groups=mesh['seq'=8,'ch'=4] {'seq'}, dimensions={0} | all-to-all | bytes 589824 | tf_op jit(solution)/shard_map/all_to_all | solution.py:633
  41.3 0.8 %shard_map.152 = (bf16[3,32,1024]{2,1,0:T(8,128)(2,1)}, f32[3,3,32]{2,1,0:T(4,128)}, f32[32,64]{1,0:T(8,128)}, f32[32,64]{1,0:T(8,128)}) custom-call(bf16[8,16,1152]{2,1,0:T(8,128)(2,1)S(1)} %all_to_all.10.recv_ref), custom_call_target="tpu_custom_call" | custom-call | tf_op jit(solution)/shard_map/pallas_call | solution.py:634
Async XLA Ops:
  2.3 16.2 %all-to-all-start = ((bf16[8,16,1024]{2,1,0:T(8,128)(2,1)}), bf16[8,16,1024]{2,1,0:T(8,128)(2,1)S(1)}, u32[]{:S(2)}, u32[]{:S(2)}) async-start(bf16[8,16,1024]{2,1,0:T(8,128)(2,1)} %shard_map.148), calls=%async_computation | async-start | bytes 524288 | tf_op jit(solution)/shard_map/all_to_all | solution.py:547
  23.2 3.1 %collective-permute-start.2 = (f32[32,64]{1,0:T(8,128)S(1)}, f32[32,64]{1,0:T(8,128)S(1)}, u32[]{:S(2)}, u32[]{:S(2)}) collective-permute-start(f32[32,64]{1,0:T(8,128)S(1)} %get-tuple-element.43.refs_0_), channel_id=1, source_target_pairs={{0,3},{1,0},{2,1},{3,2},{4,7},{5,4},{6,5},{7,6},{8,11},{9,8},{10,9... | collective-permute-start | bytes 24584 | tf_op jit(solution)/shard_map/ppermute | solution.py:614
  23.3 3.8 %collective-permute-start.1 = (f32[32,64]{1,0:T(8,128)S(1)}, f32[32,64]{1,0:T(8,128)S(1)}, u32[]{:S(2)}, u32[]{:S(2)}) collective-permute-start(f32[32,64]{1,0:T(8,128)S(1)} %get-tuple-element.43.refs_0_), channel_id=1, source_target_pairs={{0,2},{1,3},{2,0},{3,1},{4,6},{5,7},{6,4},{7,5},{8,10},{9,11},{10,... | collective-permute-start | bytes 24584 | tf_op jit(solution)/shard_map/ppermute | solution.py:614
  24.9 3.2 %collective-permute-start = (f32[32,64]{1,0:T(8,128)S(1)}, f32[32,64]{1,0:T(8,128)S(1)}, u32[]{:S(2)}, u32[]{:S(2)}) collective-permute-start(f32[32,64]{1,0:T(8,128)S(1)} %get-tuple-element.43.refs_0_), channel_id=1, source_target_pairs={{0,1},{1,2},{2,3},{3,0},{4,5},{5,6},{6,7},{7,4},{8,9},{9,10},{10,1... | collective-permute-start | bytes 24584 | tf_op jit(solution)/shard_map/ppermute | solution.py:614

commit v2 on v1

--- a/solution.py
+++ b/solution.py
@@ -76,9 +76,15 @@
     even = (feature % 2 == 0)[:, None]
     near = np.where(even, np.cos(row_angle), np.sin(row_angle))
     far = np.where(even, -np.sin(row_angle), np.cos(row_angle))
+    lane = np.concatenate([np.cos(lane_angle), np.sin(lane_angle)], 0)
+    lane_high, lane_low = np_split(lane.T)
+    grad_lane = np.block([[lane_high, lane_low], [lane_high, np.zeros_like(lane_low)]])
+    grad_row = np.concatenate([near, far, near, far], 0).T
     return (
         np.concatenate([near, far], 0).astype(np.float32),
-        np.concatenate([np.cos(lane_angle), np.sin(lane_angle)], 0).astype(np.float32),
+        lane.astype(np.float32),
+        grad_lane.astype(ml_dtypes.bfloat16),
+        grad_row.astype(np.float32),
     )
 
 
@@ -219,10 +225,10 @@
 
 
 def filter_kernel(per, length, blocks, *refs):
-    given, loaded = refs[:10], refs[10:20]
-    env_ref, spec_ref = refs[20:22]
-    hidden_refs, buffers = refs[22:25], refs[25:28]
-    mod_ref, stage_ref, load_semaphores, out_semaphores = refs[28:]
+    given, loaded = refs[:12], refs[12:24]
+    env_ref, spec_ref = refs[24:26]
+    hidden_refs, buffers = refs[26:29], list(refs[29:-4])
+    mod_ref, stage_ref, load_semaphores, out_semaphores = refs[-4:]
     loads = [
         pltpu.make_async_copy(source, target, load_semaphores.at[index])
         for index, (source, target) in enumerate(zip(given, loaded, strict=True))
@@ -231,11 +237,15 @@
         load.start()
     for load in loads:
         load.wait()
-    first_ref, _, middle_ref, turn_ref, near_ref, lane_ref, in_ref, out_ref, rates_ref, _ = loaded
+    first_ref, _, middle_ref, turn_ref, near_ref, lane_ref, _, _ = loaded[:8]
+    in_ref, out_ref, rates_ref, _ = loaded[8:]
     rows = length // LANES
     block = length // blocks
     block_rows = rows // blocks
+    if blocks == 1:
+        buffers, hidden_refs = buffers + [hidden_refs[2]], hidden_refs[:2]
     sine_high_ref, sine_low_ref, cosine_ref = buffers
+    buffers = buffers[: len(hidden_refs)]
     in_high, in_low = split(in_ref[...] * 0.5)
     in_weights = jnp.concatenate([in_high, in_high, in_low], 0)
     out_high, out_low = split(own_rows(per, out_ref))
@@ -280,19 +290,24 @@
 
 def signal_kernel(per, blocks, *refs):
     recv_ref, env_ref, first_ref, last_ref, middle_ref, turn_ref = refs[:6]
-    near_ref, lane_ref, out_ref, short_ref = refs[6:10]
-    hidden_refs = refs[10:13]
-    raw_ref, mixed_ref, spec_ref, out_grad_ref, in_grad_ref = refs[13:18]
-    buffers = refs[18:21]
-    stage_ref, weighted_ref, semaphores = refs[21:]
+    lane_ref, row_ref, out_ref, short_ref, cosine_ref = refs[6:11]
+    sines = refs[11:13]
+    raw_ref, mixed_ref, spec_ref, weighted_ref, in_grad_ref = refs[13:18]
+    stage_ref, semaphores = refs[-2:]
     devices, held, tokens = recv_ref.shape
     rows = devices * tokens // LANES
     block = rows * LANES // blocks
     block_rows = rows // blocks
     step = raw_ref.shape[0] // rows
     lows = turn_ref.shape[0] // 2
-    for copy in block_copies(0, block, buffers, hidden_refs, semaphores, False):
-        copy.start()
+    ahead = []
+    if blocks == 1:
+        ahead = [
+            pltpu.make_async_copy(source, target, semaphores.at[at])
+            for at, source, target in zip((0, 1), sines, refs[18:20], strict=True)
+        ]
+        for copy in ahead:
+            copy.start()
     taps = own_columns(per, tap_rows(short_ref))
     for device in range(devices):
         for part in range(tokens // LANES):
@@ -340,56 +355,66 @@
     out_rows = own_rows(per, out_ref)
     out_rounded = out_rows.astype(BF16).astype(F32)
     weights = jnp.concatenate([out_rows, out_rows, out_rows - out_rounded], 0).astype(BF16)
-    out_grad_ref[...] = jnp.zeros_like(out_grad_ref)
+    order, features = out_ref.shape[1], lane_ref.shape[1] // 4
     in_grad_ref[...] = jnp.zeros_like(in_grad_ref)
 
     def add_block(index):
-        copies = block_copies(index, block, buffers, hidden_refs, semaphores, False)
+        cosine_here = cosine_ref
         if blocks > 1:
-
-            @pl.when(index > 0)
-            def _():
-                for copy in copies:
-                    copy.start()
-
+            cosine_here = refs[-3]
+            (copy,) = block_copies(index, block, [cosine_here], [cosine_ref], semaphores, False)
+            copy.start()
+            copy.wait()
+        parts = []
         for row in range(block_rows):
             at = pl.multiple_of((index * block_rows + row) * 8, 8)
-            weighted_ref[:, row * LANES : (row + 1) * LANES] = stage_ref[pl.ds(at, 8), :]
-        count = lane_ref.shape[0] // 2
-        feature_high, feature_low = block_features(near_ref[index], lane_ref)
-        weighted = weighted_ref[...]
-        high = weighted.astype(BF16)
-        rounded = high.astype(F32)
-        both = jnp.concatenate([weighted, weighted - rounded], 0).astype(BF16)
+            parts.append(stage_ref[pl.ds(at, 8), :])
+        weighted = jnp.concatenate(parts, 1)
+        weighted_ref[:, pl.ds(pl.multiple_of(index * block, LANES), block)] = weighted
+        rounded = weighted.astype(BF16).astype(F32)
         terms = jnp.concatenate([weighted, weighted - rounded, weighted], 0).astype(BF16)
         grad = dot_first(weights, terms)
-        for copy in copies:
-            copy.wait()
-        sine_high_ref, sine_low_ref, cosine_ref = buffers
-        total = dot_last(both, sine_high_ref[...])
-        out_grad_ref[...] += total[:8] + total[8:] + dot_last(high, sine_low_ref[...])
-        grad_high, grad_low = split(grad * cosine_ref[...])
-        total = dot_last(jnp.concatenate([feature_high, feature_low], 0), grad_high)
-        in_grad_ref[...] += total[:count] + total[count:] + dot_last(feature_high, grad_low)
+        high, low = split(grad * cosine_here[...])
+        parts = []
+        for row in range(block_rows):
+            lanes = slice(row * LANES, (row + 1) * LANES)
+            parts.append(jnp.concatenate([high[:, lanes], low[:, lanes]], 1))
+        parts = dot(jnp.concatenate(parts, 0), lane_ref[...])
+        total = jnp.zeros((order, LANES), F32)
+        factors = row_ref[pl.ds(pl.multiple_of(index * block_rows, 8), block_rows), :]
+        for row in range(block_rows):
+            total = total + parts[row * order : (row + 1) * order, :] * factors[row : row + 1, :]
+        total = total + pltpu.roll(total, 2 * features, 1)
+        total = total + pltpu.roll(total, features, 1)
+        in_grad_ref[...] += total.T[:features, :]
 
     in_blocks(blocks, add_block)
+    for copy in ahead:
+        copy.wait()
 
 
 def proj_grad_kernel(
     per,
+    blocks,
     scale,
     short_ref,
     raw_ref,
     mixed_ref,
     spec_ref,
     kernel_spec_ref,
-    out_grad_ref,
+    weighted_ref,
     last_ref,
     middle_ref,
     turn_ref,
+    high_ref,
+    low_ref,
     slab_ref,
     stage_ref,
+    high_buffer=None,
+    low_buffer=None,
+    semaphores=None,
 ):
+    order, block = high_ref.shape[0], high_ref.shape[1] // blocks
     devices, held, width = slab_ref.shape
     tokens = width - LANES
     rows = devices * tokens // LANES
@@ -445,11 +470,26 @@
         total = jnp.sum(sums[place], axis=1, keepdims=True) * scale
         for tap in range(3):
             small = jnp.where((row == 4 + place) & (lane == tap), total[tap : tap + 1, :], small)
-    order = out_grad_ref.shape[1]
-    out_grad = jnp.concatenate(
-        [out_grad_ref[...] * scale, jnp.zeros((8, LANES - order), F32)], 1
-    )
-    out_grad = jnp.concatenate([out_grad, jnp.zeros((held - 8, LANES), F32)], 0)
+    out_grad = jnp.zeros((order, 2 * LANES), F32)
+    for index in range(blocks):
+        high_here, low_here = high_ref, low_ref
+        if blocks > 1:
+            high_here, low_here = high_buffer, low_buffer
+            copies = block_copies(
+                index, block, [high_here, low_here], [high_ref, low_ref], semaphores, False
+            )
+            for copy in copies:
+                copy.start()
+            for copy in copies:
+                copy.wait()
+        weighted = weighted_ref[:, index * block : (index + 1) * block]
+        rounded = weighted.astype(BF16).astype(F32)
+        both = jnp.concatenate([weighted, weighted - rounded], 0).astype(BF16)
+        total = dot_last(high_here[...], both)
+        total = total[:, :8] + total[:, 8:] + dot_last(low_here[...], both)[:, :8]
+        out_grad = out_grad + jnp.concatenate([total, jnp.zeros((order, 2 * LANES - 8), F32)], 1)
+    out_grad = jnp.concatenate([out_grad[:, :LANES], jnp.zeros((LANES - order, LANES), F32)], 0)
+    out_grad = out_grad.T[:held, :] * scale
     small = jnp.where(row < per, out_grad, small)
     rest = pltpu.roll(small - small.astype(BF16).astype(F32), LANES // 2, 1)
     small = jnp.where(lane < LANES // 2, small, rest).astype(BF16)
@@ -531,7 +571,10 @@
     per = max(1, channels // devices)
     held = 4 * per
     step = max(8, held)
-    small = length * order * 8 <= 8 * MIB
+    slab_rows = max(16, held)
+    blocks = max(1, rows // 64)
+    block = length // blocks
+    small = blocks == 1
     limit = (24 if small else 56) * MIB
     sds = jax.ShapeDtypeStruct
     made = pltpu.VMEM if small else sds
@@ -540,21 +583,21 @@
 
     packed = call(
         functools.partial(pack_kernel, per),
-        made((devices, held, tokens), BF16),
+        sds((devices, held, tokens), BF16),
         limit,
-        in_specs=[vmem, vmem],
+        in_specs=[vmem] * 2,
     )(keep(proj), keep(cotangent))
     recv = lax.all_to_all(packed, "seq", split_axis=0, concat_axis=0, tiled=True)
 
-    near, lane_table = feature_tables(length, features)
-    blocks = max(1, rows // 64)
-    block = length // blocks
+    near, *lane_tables = feature_tables(length, features)
     near = near.reshape(2 * features, blocks, rows // blocks).transpose(1, 0, 2)
     tables = transform_tables(length)
-    given = [tables[name] for name in ("first", "last", "middle", "turn")] + [near, lane_table]
+    given = [tables[name] for name in ("first", "last", "middle", "turn")]
+    given += [near, *lane_tables]
     given = [jnp.asarray(value) for value in given]
     given += [filter_in, filter_out.T, rates.reshape(1, channels), short_w.transpose(0, 2, 1)]
-    hidden = tuple(pltpu.HBM((order, length), kind) for kind in (BF16, BF16, F32))
+    hidden = tuple(pltpu.HBM((order, length), BF16) for _ in range(2))
+    hidden += ((made if small else pltpu.HBM)((order, length), F32),)
     buffers = [pltpu.VMEM((order, block), kind) for kind in (BF16, BF16, F32)]
     *loaded, envelope, kernel_spec, sine_high, sine_low, cosine = call(
         functools.partial(filter_kernel, per, length, blocks),
@@ -563,8 +606,8 @@
         + hidden,
         limit,
         in_specs=[hbm] * len(given),
-        out_specs=(vmem,) * (len(given) + 2) + (hbm,) * 3,
-        scratch_shapes=buffers
+        out_specs=(vmem,) * (len(given) + 2) + (hbm, hbm, vmem if small else hbm),
+        scratch_shapes=(buffers[:2] if small else buffers)
         + [
             pltpu.VMEM((8, block), F32),
             pltpu.VMEM((rows * 8, LANES), F32),
@@ -574,25 +617,23 @@
         flops=8 * length * order * 3 * features,
         moved=length * order * 8,
     )(*[keep(value) for value in given])
-    first, last, middle, turn, near, lane_table, _, out_rows, _, short_taps = map(put, loaded)
-
-    raw, mixed, spec, out_grad, in_grad = call(
+    first, last, middle, turn, _, _, grad_lane, grad_row = map(put, loaded[:8])
+    _, out_rows, _, short_taps = map(put, loaded[8:])
+
+    raw, mixed, spec, weighted, in_grad, *sines = call(
         functools.partial(signal_kernel, per, blocks),
         (
             made((rows * step, LANES), F32),
             made((2 * per, rows, LANES), F32),
             made((2 * per * lows, 2 * LANES), F32),
-            made((8, order), F32),
+            made((8, length), F32),
             sds((features, order), F32),
-        ),
+        )
+        + ((made((order, length), BF16),) * 2 if small else ()),
         limit,
-        in_specs=[vmem] * 10 + [hbm] * 3,
-        scratch_shapes=buffers
-        + [
-            pltpu.VMEM((rows * 8, LANES), F32),
-            pltpu.VMEM((8, block), F32),
-            pltpu.SemaphoreType.DMA((3,)),
-        ],
+        in_specs=[vmem] * 10 + [vmem if small else hbm] + [hbm] * 2,
+        scratch_shapes=([] if small else buffers[2:])
+        + [pltpu.VMEM((rows * 8, LANES), F32), pltpu.SemaphoreType.DMA((2,))],
         flops=400 * length * LANES,
     )(
         put(recv),
@@ -601,28 +642,41 @@
         last,
         middle,
         turn,
-        near,
-        lane_table,
+        grad_lane,
+        grad_row,
         out_rows,
         short_taps,
+        put(cosine) if small else keep(cosine),
         keep(sine_high),
         keep(sine_low),
-        keep(cosine),
     )
+    if not small:
+        sines = [sine_high, sine_low]
 
     others = [
         lax.ppermute(in_grad, "ch", [(i, (i + by) % groups) for i in range(groups)])
         for by in range(1, groups)
     ]
-    slab_rows = max(16, held)
     slab = call(
-        functools.partial(proj_grad_kernel, per, scale),
+        functools.partial(proj_grad_kernel, per, blocks, scale),
         made((devices, slab_rows, tokens + LANES), BF16),
         limit,
-        in_specs=[vmem] + [vmem] * 8,
-        scratch_shapes=[pltpu.VMEM((rows * slab_rows, LANES), F32)],
+        in_specs=[vmem] * 9 + [vmem if small else hbm] * 2,
+        scratch_shapes=[pltpu.VMEM((rows * slab_rows, LANES), F32)]
+        + ([] if small else [*buffers[:2], pltpu.SemaphoreType.DMA((2,))]),
         flops=400 * length * LANES,
-    )(short_taps, put(raw), put(mixed), put(spec), put(kernel_spec), put(out_grad), last, middle, turn)
+    )(
+        short_taps,
+        put(raw),
+        put(mixed),
+        put(spec),
+        put(kernel_spec),
+        put(weighted),
+        last,
+        middle,
+        turn,
+        *[put(value) if small else keep(value) for value in sines],
+    )
     slab = call(
         functools.partial(finish_kernel, scale),
         sds((devices, slab_rows, tokens + LANES), BF16),

time: 42.4 us -> 41.2 us (0.972)
  Pallas kernels: 15.3 us -> 13.3 us
  blocking collectives: 13.2 us -> 13.8 us
    pallas_call x1, Pallas kernels: 4.7 us -> 2.92 us  [shards(): call(functools.partial(signal_kernel, per, blocks), (made((rows * step, L...]
    all_to_all x1, waiting for transfers between devices: 2.23 us -> 3.03 us  [shards(): lax.all_to_all(packed, 'seq', split_axis=0, concat_axis=0, tiled=True)]
    pallas_call x1, Pallas kernels: 6.68 us -> 5.88 us  [shards(): call(functools.partial(filter_kernel, per, length, blocks), tuple((made(v...]
    pallas_call x2, Pallas kernels: 2.95 us -> 3.57 us  [the longest x1 1.88 us: shards(): call(functools.partial(proj_grad_kernel, per, blocks, scale), made((devic...]
    ppermute x3, waiting for transfers between devices: 1.73 us -> 1.12 us  [shards(): lax.ppermute(in_grad, 'ch', [(i, (i + by) % groups) for i in range(groups)])]
    all_to_all x1, blocking collectives: 13.2 us -> 13.8 us  [shards(): back = lax.all_to_all(slab, 'seq', split_axis=0, concat_axis=0, tiled=True)]
where the time goes in v2:
time: 41.2 us; the launch traced here: 41 us
  blocking collectives  13.8 us (33%)
  Pallas kernels  13.3 us (32%)
  starting transfers between devices  9.06 us (22%)
  waiting for transfers between devices  4.15 us (10%)
  between operations  0.66 us (2%)
    all_to_all x1, blocking collectives, shards(): back = lax.all_to_all(slab, 'seq', split_axis=0, concat_axis=0, tiled=True)  13.8 us
    all_to_all x1, starting transfers between devices, shards(): lax.all_to_all(packed, 'seq', split_axis=0, concat_axis=0, tiled=True)  7.25 us
    pallas_call x1, Pallas kernels, shards(): call(functools.partial(filter_kernel, per, length, blocks), tuple((made(v...  5.88 us
    all_to_all x1, waiting for transfers between devices, shards(): lax.all_to_all(packed, 'seq', split_axis=0, concat_axis=0, tiled=True)  3.03 us
    pallas_call x1, Pallas kernels, shards(): call(functools.partial(signal_kernel, per, blocks), (made((rows * step, L...  2.92 us
    pallas_call x1, Pallas kernels, shards(): call(functools.partial(proj_grad_kernel, per, blocks, scale), made((devic...  1.88 us
    ppermute x3, starting transfers between devices, shards(): lax.ppermute(in_grad, 'ch', [(i, (i + by) % groups) for i in range(groups)])  1.81 us
    pallas_call x1, Pallas kernels, shards(): call(functools.partial(pack_kernel, per), sds((devices, held, tokens), BF...  1.69 us
  transfers between devices with their start and end apart: 4, of which 3 were waited for; matrix products, arithmetic and copies ran while one was open for 0% of the time, Pallas kernels for 19%

profile of v2, /device:TPU:0, one launch (start us, length us, event | category | flops | bytes accessed | tf_op | source)
XLA Modules:
  0.0 41.0 jit_solution(3767480766264358625)
XLA Ops:
  0.6 1.7 %shard_map.166 = bf16[8,16,1024]{2,1,0:T(8,128)(2,1)} custom-call(bf16[3,32,1024]{2,1,0:T(8,128)(2,1)} %proj_ref.1, bf16[32,1024]{1,0:T(8,128)(2,1)} %cot_ref.1), custom_call_target="tpu_custom_call" | custom-call | tf_op jit(solution)/shard_map/pallas_call | solution.py:584
  2.3 7.3 %all-to-all-start = ((bf16[8,16,1024]{2,1,0:T(8,128)(2,1)}), bf16[8,16,1024]{2,1,0:T(8,128)(2,1)S(1)}, u32[]{:S(2)}, u32[]{:S(2)}) async-start(bf16[8,16,1024]{2,1,0:T(8,128)(2,1)} %shard_map.166), calls=%async_computation | async-start | bytes 524288 | tf_op jit(solution)/shard_map/all_to_all | solution.py:590
  9.6 5.9 %shard_map.165 = (bf16[144,192]{1,0:T(8,128)(2,1)S(1)}, bf16[64,432]{1,0:T(8,128)(2,1)S(1)}, bf16[512,256]{1,0:T(8,128)(2,1)S(1)}, f32[144,128]{1,0:T(8,128)S(1)...) custom-call(bf16[144,192]{1,0:T(8,128)(2,1)} %constant.16.clone.refs, ...), custom_call_target="tpu_custom_call" | custom-call | flops 402653184 | bytes 4194304 | tf_op jit(solution)/shard_map/pallas_call | solution.py:602
  15.5 3.0 %all-to-all-done.refs_0_ = bf16[8,16,1024]{2,1,0:T(8,128)(2,1)S(1)} async-done(((bf16[8,16,1024]{2,1,0:T(8,128)(2,1)}), bf16[8,16,1024]{2,1,0:T(8,128)(2,1)S(1)}, u32[]{:S(2)}, u32[]{:S(2)}) %all-to-all-start) | async-done | bytes 262176 | tf_op jit(solution)/shard_map/all_to_all | solution.py:590
  18.5 2.9 %shard_map.167 = (f32[1024,128]{1,0:T(8,128)S(1)}, f32[8,64,128]{2,1,0:T(8,128)S(1)}, f32[576,256]{1,0:T(8,128)S(1)}, f32[8,8192]{1,0:T(8,128)S(1)}, f32[32,64]{...) custom-call(bf16[8,16,1024]{2,1,0:T(8,128)(2,1)S(1)} %all-to-all-done.refs_0_, ...), custom_call_target="tpu_custom_call" | custom-call | flops 419430400 | tf_op jit(solution)/shard_map/pallas_call | solution.py:623
  21.4 0.1 collective-permute-start.2
  21.5 1.6 %collective-permute-start.1 = (f32[32,64]{1,0:T(8,128)S(1)}, f32[32,64]{1,0:T(8,128)S(1)}, u32[]{:S(2)}, u32[]{:S(2)}) collective-permute-start(f32[32,64]{1,0:T(8,128)S(1)} %get-tuple-element.47.refs_0_), channel_id=1, source_target_pairs={{0,2},{1,3},{2,0},{3,1},{4,6},{5,7},{6,4},{7,5},{8,10},{9,11},{10,... | collective-permute-start | bytes 24584 | tf_op jit(solution)/shard_map/ppermute | solution.py:657
  23.1 0.2 collective-permute-start
  23.2 1.9 %shard_map.168.slab_ref = bf16[8,16,1152]{2,1,0:T(8,128)(2,1)S(1)} custom-call(f32[3,3,32]{2,1,0:T(4,128)S(1)} %get-tuple-element.28.refs_9_.short_ref, f32[1024,128]{1,0:T(8,128)S(1)} %get-tuple-element.40.raw_ref, f32[8,64,128]{2,1,0:T(8,128)S(1)} %get-tuple-element.41.mixed_ref, f32[576,256]{1,0:T(8,128)S(1)} %get-tuple-element.42.spec_ref, ...), custom_call_target="tpu_custom_call" | custom-call | flops 419430400 | tf_op jit(solution)/shard_map/pallas_call | solution.py:660
  25.1 0.0 collective-permute-done.2.refs_3_
  25.1 0.2 collective-permute-done.1.refs_2_
  25.3 0.9 %collective-permute-done.refs_1_ = f32[32,64]{1,0:T(8,128)S(1)} collective-permute-done((f32[32,64]{1,0:T(8,128)S(1)}, f32[32,64]{1,0:T(8,128)S(1)}, u32[]{:S(2)}, u32[]{:S(2)}) %collective-permute-start) | collective-permute-done | bytes 8224 | tf_op jit(solution)/shard_map/ppermute | solution.py:657
  26.2 0.1 shard_map.169
  26.3 13.8 %all_to_all.10.recv_ref = bf16[8,16,1152]{2,1,0:T(8,128)(2,1)S(1)} all-to-all(bf16[8,16,1152]{2,1,0:T(8,128)(2,1)S(1)} %shard_map.169), channel_id=1, replica_groups=mesh['seq'=8,'ch'=4] {'seq'}, dimensions={0} | all-to-all | bytes 589824 | tf_op jit(solution)/shard_map/all_to_all | solution.py:687
  40.1 0.8 %shard_map.170 = (bf16[3,32,1024]{2,1,0:T(8,128)(2,1)}, f32[3,3,32]{2,1,0:T(4,128)}, f32[32,64]{1,0:T(8,128)}, f32[32,64]{1,0:T(8,128)}) custom-call(bf16[8,16,1152]{2,1,0:T(8,128)(2,1)S(1)} %all_to_all.10.recv_ref), custom_call_target="tpu_custom_call" | custom-call | tf_op jit(solution)/shard_map/pallas_call | solution.py:688
Async XLA Ops:
  2.3 16.2 %all-to-all-start = ((bf16[8,16,1024]{2,1,0:T(8,128)(2,1)}), bf16[8,16,1024]{2,1,0:T(8,128)(2,1)S(1)}, u32[]{:S(2)}, u32[]{:S(2)}) async-start(bf16[8,16,1024]{2,1,0:T(8,128)(2,1)} %shard_map.166), calls=%async_computation | async-start | bytes 524288 | tf_op jit(solution)/shard_map/all_to_all | solution.py:590
  21.4 3.7 %collective-permute-start.2 = (f32[32,64]{1,0:T(8,128)S(1)}, f32[32,64]{1,0:T(8,128)S(1)}, u32[]{:S(2)}, u32[]{:S(2)}) collective-permute-start(f32[32,64]{1,0:T(8,128)S(1)} %get-tuple-element.47.refs_0_), channel_id=1, source_target_pairs={{0,3},{1,0},{2,1},{3,2},{4,7},{5,4},{6,5},{7,6},{8,11},{9,8},{10,9... | collective-permute-start | bytes 24584 | tf_op jit(solution)/shard_map/ppermute | solution.py:657
  21.5 3.8 %collective-permute-start.1 = (f32[32,64]{1,0:T(8,128)S(1)}, f32[32,64]{1,0:T(8,128)S(1)}, u32[]{:S(2)}, u32[]{:S(2)}) collective-permute-start(f32[32,64]{1,0:T(8,128)S(1)} %get-tuple-element.47.refs_0_), channel_id=1, source_target_pairs={{0,2},{1,3},{2,0},{3,1},{4,6},{5,7},{6,4},{7,5},{8,10},{9,11},{10,... | collective-permute-start | bytes 24584 | tf_op jit(solution)/shard_map/ppermute | solution.py:657
  23.1 3.2 %collective-permute-start = (f32[32,64]{1,0:T(8,128)S(1)}, f32[32,64]{1,0:T(8,128)S(1)}, u32[]{:S(2)}, u32[]{:S(2)}) collective-permute-start(f32[32,64]{1,0:T(8,128)S(1)} %get-tuple-element.47.refs_0_), channel_id=1, source_target_pairs={{0,1},{1,2},{2,3},{3,0},{4,5},{5,6},{6,7},{7,4},{8,9},{9,10},{10,1... | collective-permute-start | bytes 24584 | tf_op jit(solution)/shard_map/ppermute | solution.py:657

commit v3 on v2

--- a/solution.py
+++ b/solution.py
@@ -386,7 +386,9 @@
             total = total + parts[row * order : (row + 1) * order, :] * factors[row : row + 1, :]
         total = total + pltpu.roll(total, 2 * features, 1)
         total = total + pltpu.roll(total, features, 1)
-        in_grad_ref[...] += total.T[:features, :]
+        total = total.T
+        half = features // 2
+        in_grad_ref[...] += jnp.concatenate([total[:half, :], total[half:features, :]], 1)
 
     in_blocks(blocks, add_block)
     for copy in ahead:
@@ -504,7 +506,7 @@
         total = total + part[...]
     total = total * scale
     rounded = total.astype(BF16).astype(F32)
-    halves = jnp.concatenate([total, total - rounded], 1)
+    halves = jnp.concatenate([total, total - rounded], 0)
     held = slab_ref.shape[1]
     count = halves.shape[0] // 4
     wide = jnp.concatenate([halves[4 * index : 4 * index + 4, :] for index in range(count)], 1)
@@ -541,7 +543,10 @@
     total = jnp.concatenate(
         [total[:, index * LANES : (index + 1) * LANES] for index in range(count)], 0
     )
-    in_ref[...] = total[:, :order] + total[:, order:]
+    half = features // 2
+    total = total[:half, :] + total[half:, :]
+    in_ref[:half, :] = total[:, :order]
+    in_ref[half:, :] = total[:, order:]
 
 
 def call(kernel, out, limit, in_specs=None, out_specs=None, flops=0, moved=0, **more):
@@ -627,7 +632,7 @@
             made((2 * per, rows, LANES), F32),
             made((2 * per * lows, 2 * LANES), F32),
             made((8, length), F32),
-            sds((features, order), F32),
+            sds((features // 2, 2 * order), F32),
         )
         + ((made((order, length), BF16),) * 2 if small else ()),
         limit,
@@ -654,8 +659,8 @@
         sines = [sine_high, sine_low]
 
     others = [
-        lax.ppermute(in_grad, "ch", [(i, (i + by) % groups) for i in range(groups)])
-        for by in range(1, groups)
+        lax.ppermute(in_grad, "ch", [(i, i ^ by) for i in range(groups)])
+        for by in (2,1,3)
     ]
     slab = call(
         functools.partial(proj_grad_kernel, per, blocks, scale),

time: 41.2 us -> 40.8 us (level)
  blocking collectives: 13.8 us -> 12.8 us
    all_to_all x1, blocking collectives: 13.8 us -> 12.8 us  [shards(): back = lax.all_to_all(slab, 'seq', split_axis=0, concat_axis=0, tiled=True)]
  transfers between devices with their start and end apart: 4 -> 4, of which waited for: 3 -> 2; matrix products, arithmetic and copies ran while one was open for 0% -> 0% of each run, Pallas kernels for 19% -> 19%
where the time goes in v3:
time: 40.8 us; the launch traced here: 40.5 us
  Pallas kernels  13.3 us (33%)
  blocking collectives  12.8 us (31%)
  starting transfers between devices  9.45 us (23%)
  waiting for transfers between devices  4.31 us (11%)
  between operations  0.67 us (2%)
    all_to_all x1, blocking collectives, shards(): back = lax.all_to_all(slab, 'seq', split_axis=0, concat_axis=0, tiled=True)  12.8 us
    all_to_all x1, starting transfers between devices, shards(): lax.all_to_all(packed, 'seq', split_axis=0, concat_axis=0, tiled=True)  7.25 us
    pallas_call x1, Pallas kernels, shards(): call(functools.partial(filter_kernel, per, length, blocks), tuple((made(v...  5.88 us
    all_to_all x1, waiting for transfers between devices, shards(): lax.all_to_all(packed, 'seq', split_axis=0, concat_axis=0, tiled=True)  3.03 us
    pallas_call x1, Pallas kernels, shards(): call(functools.partial(signal_kernel, per, blocks), (made((rows * step, L...  2.99 us
    ppermute x3, starting transfers between devices, shards(): lax.ppermute(in_grad, 'ch', [(i, i ^ by) for i in range(groups)])  2.2 us
    pallas_call x1, Pallas kernels, shards(): call(functools.partial(proj_grad_kernel, per, blocks, scale), made((devic...  1.85 us
    pallas_call x1, Pallas kernels, shards(): call(functools.partial(pack_kernel, per), sds((devices, held, tokens), BF...  1.69 us
  transfers between devices with their start and end apart: 4, of which 2 were waited for; matrix products, arithmetic and copies ran while one was open for 0% of the time, Pallas kernels for 19%

profile of v3, /device:TPU:0, one launch (start us, length us, event | category | flops | bytes accessed | tf_op | source)
XLA Modules:
  0.0 40.5 jit_solution(17656797980658411987)
XLA Ops:
  0.6 1.7 %shard_map.166 = bf16[8,16,1024]{2,1,0:T(8,128)(2,1)} custom-call(bf16[3,32,1024]{2,1,0:T(8,128)(2,1)} %proj_ref.1, bf16[32,1024]{1,0:T(8,128)(2,1)} %cot_ref.1), custom_call_target="tpu_custom_call" | custom-call | tf_op jit(solution)/shard_map/pallas_call | solution.py:589
  2.3 7.3 %all-to-all-start = ((bf16[8,16,1024]{2,1,0:T(8,128)(2,1)}), bf16[8,16,1024]{2,1,0:T(8,128)(2,1)S(1)}, u32[]{:S(2)}, u32[]{:S(2)}) async-start(bf16[8,16,1024]{2,1,0:T(8,128)(2,1)} %shard_map.166), calls=%async_computation | async-start | bytes 524288 | tf_op jit(solution)/shard_map/all_to_all | solution.py:595
  9.6 5.9 %shard_map.165 = (bf16[144,192]{1,0:T(8,128)(2,1)S(1)}, bf16[64,432]{1,0:T(8,128)(2,1)S(1)}, bf16[512,256]{1,0:T(8,128)(2,1)S(1)}, f32[144,128]{1,0:T(8,128)S(1)...) custom-call(bf16[144,192]{1,0:T(8,128)(2,1)} %constant.16.clone.refs, ...), custom_call_target="tpu_custom_call" | custom-call | flops 402653184 | bytes 4194304 | tf_op jit(solution)/shard_map/pallas_call | solution.py:607
  15.5 3.0 %all-to-all-done.refs_0_ = bf16[8,16,1024]{2,1,0:T(8,128)(2,1)S(1)} async-done(((bf16[8,16,1024]{2,1,0:T(8,128)(2,1)}), bf16[8,16,1024]{2,1,0:T(8,128)(2,1)S(1)}, u32[]{:S(2)}, u32[]{:S(2)}) %all-to-all-start) | async-done | bytes 262176 | tf_op jit(solution)/shard_map/all_to_all | solution.py:595
  18.5 3.0 %shard_map.167 = (f32[1024,128]{1,0:T(8,128)S(1)}, f32[8,64,128]{2,1,0:T(8,128)S(1)}, f32[576,256]{1,0:T(8,128)S(1)}, f32[8,8192]{1,0:T(8,128)S(1)}, f32[16,128]...) custom-call(bf16[8,16,1024]{2,1,0:T(8,128)(2,1)S(1)} %all-to-all-done.refs_0_, ...), custom_call_target="tpu_custom_call" | custom-call | flops 419430400 | tf_op jit(solution)/shard_map/pallas_call | solution.py:628
  21.5 0.1 collective-permute-start.2
  21.6 1.6 %collective-permute-start.1 = (f32[16,128]{1,0:T(8,128)S(1)}, f32[16,128]{1,0:T(8,128)S(1)}, u32[]{:S(2)}, u32[]{:S(2)}) collective-permute-start(f32[16,128]{1,0:T(8,128)S(1)} %get-tuple-element.47.refs_0_), channel_id=1, source_target_pairs={{0,1},{1,0},{2,3},{3,2},{4,5},{5,4},{6,7},{7,6},{8,9},{9,8},{10,11... | collective-permute-start | bytes 24584 | tf_op jit(solution)/shard_map/ppermute | solution.py:662
  23.2 0.5 %collective-permute-start = (f32[16,128]{1,0:T(8,128)S(1)}, f32[16,128]{1,0:T(8,128)S(1)}, u32[]{:S(2)}, u32[]{:S(2)}) collective-permute-start(f32[16,128]{1,0:T(8,128)S(1)} %get-tuple-element.47.refs_0_), channel_id=1, source_target_pairs={{0,2},{1,3},{2,0},{3,1},{4,6},{5,7},{6,4},{7,5},{8,10},{9,11},{10,... | collective-permute-start | bytes 24584 | tf_op jit(solution)/shard_map/ppermute | solution.py:662
  23.7 1.9 %shard_map.168.slab_ref = bf16[8,16,1152]{2,1,0:T(8,128)(2,1)S(1)} custom-call(f32[3,3,32]{2,1,0:T(4,128)S(1)} %get-tuple-element.28.refs_9_.short_ref, f32[1024,128]{1,0:T(8,128)S(1)} %get-tuple-element.40.raw_ref, f32[8,64,128]{2,1,0:T(8,128)S(1)} %get-tuple-element.41.mixed_ref, f32[576,256]{1,0:T(8,128)S(1)} %get-tuple-element.42.spec_ref, ...), custom_call_target="tpu_custom_call" | custom-call | flops 419430400 | tf_op jit(solution)/shard_map/pallas_call | solution.py:665
  25.6 0.0 collective-permute-done.2.refs_3_
  25.6 0.0 collective-permute-done.1.refs_2_
  25.6 1.3 %collective-permute-done.refs_1_ = f32[16,128]{1,0:T(8,128)S(1)} collective-permute-done((f32[16,128]{1,0:T(8,128)S(1)}, f32[16,128]{1,0:T(8,128)S(1)}, u32[]{:S(2)}, u32[]{:S(2)}) %collective-permute-start) | collective-permute-done | bytes 8224 | tf_op jit(solution)/shard_map/ppermute | solution.py:662
  26.9 12.8 %all_to_all.10.recv_ref = bf16[8,16,1152]{2,1,0:T(8,128)(2,1)S(1)} all-to-all(bf16[8,16,1152]{2,1,0:T(8,128)(2,1)S(1)} %shard_map.169), channel_id=1, replica_groups=mesh['seq'=8,'ch'=4] {'seq'}, dimensions={0} | all-to-all | bytes 589824 | tf_op jit(solution)/shard_map/all_to_all | solution.py:692
  39.6 0.8 %shard_map.170 = (bf16[3,32,1024]{2,1,0:T(8,128)(2,1)}, f32[3,3,32]{2,1,0:T(4,128)}, f32[32,64]{1,0:T(8,128)}, f32[32,64]{1,0:T(8,128)}) custom-call(bf16[8,16,1152]{2,1,0:T(8,128)(2,1)S(1)} %all_to_all.10.recv_ref), custom_call_target="tpu_custom_call" | custom-call | tf_op jit(solution)/shard_map/pallas_call | solution.py:693
  (1 shorter events, 0.0 us)
Async XLA Ops:
  2.3 16.2 %all-to-all-start = ((bf16[8,16,1024]{2,1,0:T(8,128)(2,1)}), bf16[8,16,1024]{2,1,0:T(8,128)(2,1)S(1)}, u32[]{:S(2)}, u32[]{:S(2)}) async-start(bf16[8,16,1024]{2,1,0:T(8,128)(2,1)} %shard_map.166), calls=%async_computation | async-start | bytes 524288 | tf_op jit(solution)/shard_map/all_to_all | solution.py:595
  21.5 4.1 %collective-permute-start.2 = (f32[16,128]{1,0:T(8,128)S(1)}, f32[16,128]{1,0:T(8,128)S(1)}, u32[]{:S(2)}, u32[]{:S(2)}) collective-permute-start(f32[16,128]{1,0:T(8,128)S(1)} %get-tuple-element.47.refs_0_), channel_id=1, source_target_pairs={{0,3},{1,2},{2,1},{3,0},{4,7},{5,6},{6,5},{7,4},{8,11},{9,10},{10,... | collective-permute-start | bytes 24584 | tf_op jit(solution)/shard_map/ppermute | solution.py:662
  21.6 4.0 %collective-permute-start.1 = (f32[16,128]{1,0:T(8,128)S(1)}, f32[16,128]{1,0:T(8,128)S(1)}, u32[]{:S(2)}, u32[]{:S(2)}) collective-permute-start(f32[16,128]{1,0:T(8,128)S(1)} %get-tuple-element.47.refs_0_), channel_id=1, source_target_pairs={{0,1},{1,0},{2,3},{3,2},{4,5},{5,4},{6,7},{7,6},{8,9},{9,8},{10,11... | collective-permute-start | bytes 24584 | tf_op jit(solution)/shard_map/ppermute | solution.py:662
  23.2 3.7 %collective-permute-start = (f32[16,128]{1,0:T(8,128)S(1)}, f32[16,128]{1,0:T(8,128)S(1)}, u32[]{:S(2)}, u32[]{:S(2)}) collective-permute-start(f32[16,128]{1,0:T(8,128)S(1)} %get-tuple-element.47.refs_0_), channel_id=1, source_target_pairs={{0,2},{1,3},{2,0},{3,1},{4,6},{5,7},{6,4},{7,5},{8,10},{9,11},{10,... | collective-permute-start | bytes 24584 | tf_op jit(solution)/shard_map/ppermute | solution.py:662

commit v4 on v3

--- a/solution.py
+++ b/solution.py
@@ -417,9 +417,10 @@
     semaphores=None,
 ):
     order, block = high_ref.shape[0], high_ref.shape[1] // blocks
-    devices, held, width = slab_ref.shape
-    tokens = width - LANES
-    rows = devices * tokens // LANES
+    devices = slab_ref.shape[0]
+    rows = weighted_ref.shape[1] // LANES
+    tokens = rows // devices * LANES
+    held = stage_ref.shape[0] // rows
     taps = own_columns(per, tap_rows(short_ref))
     step = raw_ref.shape[0] // rows
     lows = turn_ref.shape[0] // 2
@@ -459,19 +460,29 @@
                 parts.append(jnp.sum(grad * base, axis=0, keepdims=True))
             sums[index * per + channel] = jnp.concatenate(parts, 0)
             stage_ref[pl.ds(index * per + channel, rows, stride=held), :] = total
+    parts = tokens // LANES
     for device in range(devices):
-        for part in range(tokens // LANES):
-            at = (device * (tokens // LANES) + part) * held
-            slab_ref[device, :, part * LANES : (part + 1) * LANES] = stage_ref[
-                at : at + held, :
-            ].astype(BF16)
-    row = lax.broadcasted_iota(jnp.int32, (held, LANES), 0)
-    lane = lax.broadcasted_iota(jnp.int32, (held, LANES), 1)
-    small = jnp.zeros((held, LANES), F32)
+        blocks_here = []
+        for part in range(parts):
+            at = (device * parts + part) * held
+            blocks_here.append(stage_ref[at : at + held, :])
+        for part in range(parts):
+            lanes = slice(part * LANES, (part + 1) * LANES)
+            slab_ref[device, :, lanes] = blocks_here[part][:8, :].astype(BF16)
+        if held > 8:
+            for part in range(parts // 2):
+                lanes = slice(tokens + part * LANES, tokens + (part + 1) * LANES)
+                pair = [blocks_here[part][8:12, :], blocks_here[part + parts // 2][8:12, :]]
+                slab_ref[device, :, lanes] = jnp.concatenate(pair, 0).astype(BF16)
+    row = lax.broadcasted_iota(jnp.int32, (8, LANES), 0)
+    lane = lax.broadcasted_iota(jnp.int32, (8, LANES), 1)
+    small = jnp.zeros((8, LANES), F32)
     for place in range(3 * per):
+        index, channel = place // per, place % per
         total = jnp.sum(sums[place], axis=1, keepdims=True) * scale
         for tap in range(3):
-            small = jnp.where((row == 4 + place) & (lane == tap), total[tap : tap + 1, :], small)
+            at = (row == per + channel) & (lane == 3 * index + tap)
+            small = jnp.where(at, total[tap : tap + 1, :], small)
     out_grad = jnp.zeros((order, 2 * LANES), F32)
     for index in range(blocks):
         high_here, low_here = high_ref, low_ref
@@ -491,60 +502,65 @@
         total = total[:, :8] + total[:, 8:] + dot_last(low_here[...], both)[:, :8]
         out_grad = out_grad + jnp.concatenate([total, jnp.zeros((order, 2 * LANES - 8), F32)], 1)
     out_grad = jnp.concatenate([out_grad[:, :LANES], jnp.zeros((LANES - order, LANES), F32)], 0)
-    out_grad = out_grad.T[:held, :] * scale
+    out_grad = out_grad.T[:8, :] * scale
     small = jnp.where(row < per, out_grad, small)
     rest = pltpu.roll(small - small.astype(BF16).astype(F32), LANES // 2, 1)
     small = jnp.where(lane < LANES // 2, small, rest).astype(BF16)
     for device in range(devices):
-        slab_ref[device, :, tokens:] = small
+        slab_ref[device, :, slab_ref.shape[2] - LANES :] = small
 
 
 def finish_kernel(scale, slab_ref, *refs):
-    parts, result_ref = refs[:-1], refs[-1]
-    total = parts[0][...]
-    for part in parts[1:]:
-        total = total + part[...]
-    total = total * scale
-    rounded = total.astype(BF16).astype(F32)
-    halves = jnp.concatenate([total, total - rounded], 0)
-    held = slab_ref.shape[1]
-    count = halves.shape[0] // 4
-    wide = jnp.concatenate([halves[4 * index : 4 * index + 4, :] for index in range(count)], 1)
-    wide = jnp.concatenate([jnp.zeros((held - 4, wide.shape[1]), F32), wide], 0)
-    keep = lax.broadcasted_iota(jnp.int32, wide.shape, 0) < held - 4
+    parts, result_ref = [ref[...] for ref in refs[:-1]], refs[-1]
+    while len(parts) > 1:
+        parts = [parts[at] + parts[at + 1] for at in range(0, len(parts), 2)]
+    total = parts[0] * scale
+    halves = jnp.concatenate([total, total - total.astype(BF16).astype(F32)], 0)
+    count = halves.shape[0] // 8
+    wide = jnp.concatenate([halves[8 * index : 8 * index + 8, :] for index in range(count)], 1)
+    wide = wide.astype(BF16)
+    start, end = slab_ref.shape[2] - (count + 1) * LANES, slab_ref.shape[2] - LANES
     for device in range(slab_ref.shape[0]):
-        main = slab_ref[device, :, : wide.shape[1]].astype(F32)
-        result_ref[device, :, : wide.shape[1]] = jnp.where(keep, main, wide).astype(BF16)
-        result_ref[device, :, wide.shape[1] :] = slab_ref[device, :, wide.shape[1] :]
-
-
-def unpack_kernel(per, recv_ref, proj_ref, short_ref, out_ref, in_ref):
+        result_ref[device, :, :start] = slab_ref[device, :, :start]
+        result_ref[device, :, start:end] = wide
+        result_ref[device, :, end:] = slab_ref[device, :, end:]
+
+
+def unpack_kernel(per, recv_ref, proj_ref, short_ref, out_ref):
     channels, tokens = proj_ref.shape[1:]
     devices = channels // per
-    held = recv_ref.shape[1]
-    features, order = in_ref.shape
+    order = out_ref.shape[1]
+    slabs = [recv_ref[device].astype(F32) for device in range(devices)]
     for index in range(3):
-        rows = [
-            recv_ref[device, index * per : (index + 1) * per, :tokens].astype(F32)
-            for device in range(devices)
-        ]
+        rows = []
+        for slab in slabs:
+            if index * per < 8:
+                rows.append(slab[index * per : (index + 1) * per, :tokens])
+            else:
+                lanes = slice(tokens, tokens + tokens // 2)
+                rows.append(jnp.concatenate([slab[:per, lanes], slab[per : 2 * per, lanes]], 1))
         proj_ref[index] = jnp.concatenate(rows, 0).astype(BF16)
-    small = [recv_ref[device, :, tokens:].astype(F32) for device in range(devices)]
+    small = [slab[:, slab.shape[1] - LANES :] for slab in slabs]
     small = [part + pltpu.roll(part, LANES // 2, 1) for part in small]
+    out_ref[...] = jnp.concatenate([part[:per, :order] for part in small], 0)
+    rows = jnp.concatenate([part[per : 2 * per, :] for part in small], 0).T
     for index in range(3):
-        at = 4 + index * per
-        rows = jnp.concatenate([part[at : at + per, :] for part in small], 0)
-        short_ref[index] = rows.T[:3, :]
-    out_ref[...] = jnp.concatenate([part[:per, :order] for part in small], 0)
-    count = features // 4
-    total = recv_ref[0, held - 4 :, : count * LANES].astype(F32)
-    for device in range(1, devices):
-        total = total + recv_ref[device, held - 4 :, : count * LANES].astype(F32)
-    total = jnp.concatenate(
-        [total[:, index * LANES : (index + 1) * LANES] for index in range(count)], 0
-    )
-    half = features // 2
-    total = total[:half, :] + total[half:, :]
+        short_ref[index] = rows[3 * index : 3 * index + 3, :]
+
+
+def in_sum_kernel(sources, recv_ref, sum_ref):
+    count = sum_ref.shape[0] // 4
+    start = recv_ref.shape[2] - (count + 1) * LANES
+    total = recv_ref[0, :, start : start + count * LANES].astype(F32)
+    for source in range(1, sources):
+        total = total + recv_ref[source, :, start : start + count * LANES].astype(F32)
+    total = [total[:, index * LANES : (index + 1) * LANES] for index in range(count)]
+    sum_ref[...] = jnp.concatenate(total[: count // 2], 0) + jnp.concatenate(total[count // 2 :], 0)
+
+
+def in_grad_kernel(own_ref, other_ref, in_ref):
+    half, order = in_ref.shape[0] // 2, in_ref.shape[1]
+    total = own_ref[...] + other_ref[...]
     in_ref[:half, :] = total[:, :order]
     in_ref[half:, :] = total[:, order:]
 
@@ -576,7 +592,7 @@
     per = max(1, channels // devices)
     held = 4 * per
     step = max(8, held)
-    slab_rows = max(16, held)
+    width = tokens if 3 * per <= 8 else tokens + tokens // 2
     blocks = max(1, rows // 64)
     block = length // blocks
     small = blocks == 1
@@ -658,16 +674,20 @@
     if not small:
         sines = [sine_high, sine_low]
 
-    others = [
-        lax.ppermute(in_grad, "ch", [(i, i ^ by) for i in range(groups)])
-        for by in (2,1,3)
-    ]
+    def exchange(value, by):
+        return lax.ppermute(value, "ch", [(i, i ^ by) for i in range(groups)])
+
+    steps = [1 << step for step in range(1, groups.bit_length() - 1)][::-1]
+    for by in steps[:-1]:
+        in_grad = in_grad + exchange(in_grad, by)
+    others = [exchange(in_grad, by) for by in steps[-1:]]
+    shape = (devices, 8, width + features // 8 * LANES + LANES)
     slab = call(
         functools.partial(proj_grad_kernel, per, blocks, scale),
-        made((devices, slab_rows, tokens + LANES), BF16),
+        made(shape, BF16),
         limit,
         in_specs=[vmem] * 9 + [vmem if small else hbm] * 2,
-        scratch_shapes=[pltpu.VMEM((rows * slab_rows, LANES), F32)]
+        scratch_shapes=[pltpu.VMEM((rows * max(8, held), LANES), F32)]
         + ([] if small else [*buffers[:2], pltpu.SemaphoreType.DMA((2,))]),
         flops=400 * length * LANES,
     )(
@@ -684,23 +704,35 @@
     )
     slab = call(
         functools.partial(finish_kernel, scale),
-        sds((devices, slab_rows, tokens + LANES), BF16),
+        sds(shape, BF16),
         limit,
-        in_specs=[vmem] * (groups + 1),
+        in_specs=[vmem] * (2 + len(others)),
     )(put(slab), in_grad, *others)
 
     back = lax.all_to_all(slab, "seq", split_axis=0, concat_axis=0, tiled=True)
-    grad_proj, grad_short, grad_out, grad_in = call(
+    in_sum = call(
+        functools.partial(in_sum_kernel, channels // per),
+        made((features // 2, 2 * order), F32),
+        limit,
+        in_specs=[vmem],
+    )(back)
+    in_other = exchange(in_sum, 1)
+    grad_proj, grad_short, grad_out = call(
         functools.partial(unpack_kernel, per),
         (
             sds((3, channels, tokens), BF16),
             sds((3, 3, channels), F32),
             sds((channels, order), F32),
-            sds((features, order), F32),
         ),
         limit,
         in_specs=[vmem],
     )(back)
+    grad_in = call(
+        in_grad_kernel,
+        sds((features, order), F32),
+        limit,
+        in_specs=[vmem] * 2,
+    )(put(in_sum), in_other)
     return grad_proj, grad_short.transpose(0, 2, 1), grad_out.T, grad_in
 
 

time: 40.8 us -> 40.1 us (0.983)
  Pallas kernels: 13.3 us -> 14 us
  waiting for transfers between devices: 4.31 us -> 3.64 us
  starting transfers between devices: 9.45 us -> 8.91 us
    pallas_call x2 -> x4, Pallas kernels: 1.89 us -> 2.57 us  [the longest x1 1.86 us: shards(): call(functools.partial(proj_grad_kernel, per, blocks, scale), made(shape,...]
    ppermute x3 -> x2, waiting for transfers between devices: 1.28 us -> 0.62 us  [exchange(): return lax.ppermute(value, 'ch', [(i, i ^ by) for i in range(groups)])]
    ppermute x3 -> x2, starting transfers between devices: 2.2 us -> 1.65 us  [exchange(): return lax.ppermute(value, 'ch', [(i, i ^ by) for i in range(groups)])]
  transfers between devices with their start and end apart: 4 -> 3, of which waited for: 2 -> 3; matrix products, arithmetic and copies ran while one was open for 0% -> 0% of each run, Pallas kernels for 19% -> 22%
where the time goes in v4:
time: 40.1 us; the launch traced here: 39.8 us
  Pallas kernels  14 us (35%)
  blocking collectives  12.7 us (32%)
  starting transfers between devices  8.91 us (22%)
  waiting for transfers between devices  3.64 us (9%)
  between operations  0.67 us (2%)
    all_to_all x1, blocking collectives, shards(): back = lax.all_to_all(slab, 'seq', split_axis=0, concat_axis=0, tiled=True)  12.7 us
    all_to_all x1, starting transfers between devices, shards(): lax.all_to_all(packed, 'seq', split_axis=0, concat_axis=0, tiled=True)  7.25 us
    pallas_call x1, Pallas kernels, shards(): call(functools.partial(filter_kernel, per, length, blocks), tuple((made(v...  5.89 us
    all_to_all x1, waiting for transfers between devices, shards(): lax.all_to_all(packed, 'seq', split_axis=0, concat_axis=0, tiled=True)  3.02 us
    pallas_call x1, Pallas kernels, shards(): call(functools.partial(signal_kernel, per, blocks), (made((rows * step, L...  2.99 us
    pallas_call x1, Pallas kernels, shards(): call(functools.partial(proj_grad_kernel, per, blocks, scale), made(shape,...  1.86 us
    pallas_call x1, Pallas kernels, shards(): call(functools.partial(pack_kernel, per), sds((devices, held, tokens), BF...  1.69 us
    ppermute x2, starting transfers between devices, exchange(): return lax.ppermute(value, 'ch', [(i, i ^ by) for i in range(groups)])  1.65 us
  transfers between devices with their start and end apart: 3, of which 3 were waited for; matrix products, arithmetic and copies ran while one was open for 0% of the time, Pallas kernels for 22%

profile of v4, /device:TPU:0, one launch (start us, length us, event | category | flops | bytes accessed | tf_op | source)
XLA Modules:
  0.0 39.8 jit_solution(2641389463475652467)
XLA Ops:
  0.6 1.7 %shard_map.166 = bf16[8,16,1024]{2,1,0:T(8,128)(2,1)} custom-call(bf16[3,32,1024]{2,1,0:T(8,128)(2,1)} %proj_ref.1, bf16[32,1024]{1,0:T(8,128)(2,1)} %cot_ref.1), custom_call_target="tpu_custom_call" | custom-call | tf_op jit(solution)/shard_map/pallas_call | solution.py:605
  2.3 7.3 %all-to-all-start = ((bf16[8,16,1024]{2,1,0:T(8,128)(2,1)}), bf16[8,16,1024]{2,1,0:T(8,128)(2,1)S(1)}, u32[]{:S(2)}, u32[]{:S(2)}) async-start(bf16[8,16,1024]{2,1,0:T(8,128)(2,1)} %shard_map.166), calls=%async_computation | async-start | bytes 524288 | tf_op jit(solution)/shard_map/all_to_all | solution.py:611
  9.6 5.9 %shard_map.165 = (bf16[144,192]{1,0:T(8,128)(2,1)S(1)}, bf16[64,432]{1,0:T(8,128)(2,1)S(1)}, bf16[512,256]{1,0:T(8,128)(2,1)S(1)}, f32[144,128]{1,0:T(8,128)S(1)...) custom-call(bf16[144,192]{1,0:T(8,128)(2,1)} %constant.16.clone.refs, ...), custom_call_target="tpu_custom_call" | custom-call | flops 402653184 | bytes 4194304 | tf_op jit(solution)/shard_map/pallas_call | solution.py:623
  15.5 3.0 %all-to-all-done.refs_0_ = bf16[8,16,1024]{2,1,0:T(8,128)(2,1)S(1)} async-done(((bf16[8,16,1024]{2,1,0:T(8,128)(2,1)}), bf16[8,16,1024]{2,1,0:T(8,128)(2,1)S(1)}, u32[]{:S(2)}, u32[]{:S(2)}) %all-to-all-start) | async-done | bytes 262176 | tf_op jit(solution)/shard_map/all_to_all | solution.py:611
  18.5 3.0 %shard_map.167 = (f32[1024,128]{1,0:T(8,128)S(1)}, f32[8,64,128]{2,1,0:T(8,128)S(1)}, f32[576,256]{1,0:T(8,128)S(1)}, f32[8,8192]{1,0:T(8,128)S(1)}, f32[16,128]...) custom-call(bf16[8,16,1024]{2,1,0:T(8,128)(2,1)S(1)} %all-to-all-done.refs_0_, ...), custom_call_target="tpu_custom_call" | custom-call | flops 419430400 | tf_op jit(solution)/shard_map/pallas_call | solution.py:644
  21.5 1.6 %collective-permute-start = (f32[16,128]{1,0:T(8,128)S(1)}, f32[16,128]{1,0:T(8,128)S(1)}, u32[]{:S(2)}, u32[]{:S(2)}) collective-permute-start(f32[16,128]{1,0:T(8,128)S(1)} %get-tuple-element.46.refs_0_), channel_id=1, source_target_pairs={{0,2},{1,3},{2,0},{3,1},{4,6},{5,7},{6,4},{7,5},{8,10},{9,11},{10,... | collective-permute-start | bytes 24584 | tf_op jit(solution)/shard_map/ppermute | solution.py:678
  23.1 1.9 %shard_map.168.slab_ref = bf16[8,8,2176]{2,1,0:T(8,128)(2,1)S(1)} custom-call(f32[3,3,32]{2,1,0:T(4,128)S(1)} %get-tuple-element.27.refs_9_.short_ref, f32[1024,128]{1,0:T(8,128)S(1)} %get-tuple-element.39.raw_ref, f32[8,64,128]{2,1,0:T(8,128)S(1)} %get-tuple-element.40.mixed_ref, f32[576,256]{1,0:T(8,128)S(1)} %get-tuple-element.41.spec_ref, ...), custom_call_target="tpu_custom_call" | custom-call | flops 419430400 | tf_op jit(solution)/shard_map/pallas_call | solution.py:685
  24.9 0.3 collective-permute-done.refs_1_
  25.2 12.7 %all_to_all.10.recv_ref = bf16[8,8,2176]{2,1,0:T(8,128)(2,1)S(1)} all-to-all(bf16[8,8,2176]{2,1,0:T(8,128)(2,1)S(1)} %shard_map.169), channel_id=1, replica_groups=mesh['seq'=8,'ch'=4] {'seq'}, dimensions={0} | all-to-all | bytes 557056 | tf_op jit(solution)/shard_map/all_to_all | solution.py:712
  37.9 0.1 collective-permute-start.1
  38.0 0.8 %shard_map.170 = (bf16[3,32,1024]{2,1,0:T(8,128)(2,1)}, f32[3,3,32]{2,1,0:T(4,128)}, f32[32,64]{1,0:T(8,128)}) custom-call(bf16[8,8,2176]{2,1,0:T(8,128)(2,1)S(1)} %all_to_all.10.recv_ref), custom_call_target="tpu_custom_call" | custom-call | tf_op jit(solution)/shard_map/pallas_call | solution.py:720
  38.8 0.3 collective-permute-done.1.other_ref
  39.1 0.7 %shard_map.172 = f32[32,64]{1,0:T(8,128)} custom-call(f32[16,128]{1,0:T(8,128)S(1)} %shard_map.171.own_ref, f32[16,128]{1,0:T(8,128)S(1)} %collective-permute-done.1.other_ref), custom_call_target="tpu_custom_call" | custom-call | tf_op jit(solution)/shard_map/pallas_call | solution.py:730
  (2 shorter events, 0.0 us)
Async XLA Ops:
  2.3 16.2 %all-to-all-start = ((bf16[8,16,1024]{2,1,0:T(8,128)(2,1)}), bf16[8,16,1024]{2,1,0:T(8,128)(2,1)S(1)}, u32[]{:S(2)}, u32[]{:S(2)}) async-start(bf16[8,16,1024]{2,1,0:T(8,128)(2,1)} %shard_map.166), calls=%async_computation | async-start | bytes 524288 | tf_op jit(solution)/shard_map/all_to_all | solution.py:611
  21.5 3.7 %collective-permute-start = (f32[16,128]{1,0:T(8,128)S(1)}, f32[16,128]{1,0:T(8,128)S(1)}, u32[]{:S(2)}, u32[]{:S(2)}) collective-permute-start(f32[16,128]{1,0:T(8,128)S(1)} %get-tuple-element.46.refs_0_), channel_id=1, source_target_pairs={{0,2},{1,3},{2,0},{3,1},{4,6},{5,7},{6,4},{7,5},{8,10},{9,11},{10,... | collective-permute-start | bytes 24584 | tf_op jit(solution)/shard_map/ppermute | solution.py:678
  37.9 1.2 %collective-permute-start.1 = (f32[16,128]{1,0:T(8,128)S(1)}, f32[16,128]{1,0:T(8,128)S(1)}, u32[]{:S(2)}, u32[]{:S(2)}) collective-permute-start(f32[16,128]{1,0:T(8,128)S(1)} %shard_map.171.own_ref), channel_id=1, source_target_pairs={{0,1},{1,0},{2,3},{3,2},{4,5},{5,4},{6,7},{7,6},{8,9},{9,8},{10,11... | collective-permute-start | bytes 24584 | tf_op jit(solution)/shard_map/ppermute | solution.py:678

commit v5 on v4

--- a/solution.py
+++ b/solution.py
@@ -356,7 +356,8 @@
     out_rounded = out_rows.astype(BF16).astype(F32)
     weights = jnp.concatenate([out_rows, out_rows, out_rows - out_rounded], 0).astype(BF16)
     order, features = out_ref.shape[1], lane_ref.shape[1] // 4
-    in_grad_ref[...] = jnp.zeros_like(in_grad_ref)
+    if blocks > 1:
+        in_grad_ref[...] = jnp.zeros_like(in_grad_ref)
 
     def add_block(index):
         cosine_here = cosine_ref
@@ -380,15 +381,24 @@
             lanes = slice(row * LANES, (row + 1) * LANES)
             parts.append(jnp.concatenate([high[:, lanes], low[:, lanes]], 1))
         parts = dot(jnp.concatenate(parts, 0), lane_ref[...])
-        total = jnp.zeros((order, LANES), F32)
         factors = row_ref[pl.ds(pl.multiple_of(index * block_rows, 8), block_rows), :]
-        for row in range(block_rows):
-            total = total + parts[row * order : (row + 1) * order, :] * factors[row : row + 1, :]
+        totals = []
+        height = order // 2
+        for start in range(0, order, height):
+            total = jnp.zeros((height, LANES), F32)
+            for row in range(block_rows):
+                at = row * order + start
+                total = total + parts[at : at + height, :] * factors[row : row + 1, :]
+            totals.append(total)
+        total = jnp.concatenate(totals, 0)
         total = total + pltpu.roll(total, 2 * features, 1)
         total = total + pltpu.roll(total, features, 1)
         total = total.T
         half = features // 2
-        in_grad_ref[...] += jnp.concatenate([total[:half, :], total[half:features, :]], 1)
+        total = jnp.concatenate([total[:half, :], total[half:features, :]], 1)
+        if blocks > 1:
+            total = total + in_grad_ref[...]
+        in_grad_ref[...] = total
 
     in_blocks(blocks, add_block)
     for copy in ahead:

time: 40.1 us -> 40.1 us (level)
  no operation moved by 1% of the time
where the time goes in v5:
time: 40.1 us; the launch traced here: 39.8 us
  Pallas kernels  14 us (35%)
  blocking collectives  12.7 us (32%)
  starting transfers between devices  8.91 us (22%)
  waiting for transfers between devices  3.64 us (9%)
  between operations  0.67 us (2%)
    all_to_all x1, blocking collectives, shards(): back = lax.all_to_all(slab, 'seq', split_axis=0, concat_axis=0, tiled=True)  12.7 us
    all_to_all x1, starting transfers between devices, shards(): lax.all_to_all(packed, 'seq', split_axis=0, concat_axis=0, tiled=True)  7.25 us
    pallas_call x1, Pallas kernels, shards(): call(functools.partial(filter_kernel, per, length, blocks), tuple((made(v...  5.89 us
    all_to_all x1, waiting for transfers between devices, shards(): lax.all_to_all(packed, 'seq', split_axis=0, concat_axis=0, tiled=True)  3.02 us
    pallas_call x1, Pallas kernels, shards(): call(functools.partial(signal_kernel, per, blocks), (made((rows * step, L...  2.99 us
    pallas_call x1, Pallas kernels, shards(): call(functools.partial(proj_grad_kernel, per, blocks, scale), made(shape,...  1.86 us
    pallas_call x1, Pallas kernels, shards(): call(functools.partial(pack_kernel, per), sds((devices, held, tokens), BF...  1.69 us
    ppermute x2, starting transfers between devices, exchange(): return lax.ppermute(value, 'ch', [(i, i ^ by) for i in range(groups)])  1.65 us
  transfers between devices with their start and end apart: 3, of which 3 were waited for; matrix products, arithmetic and copies ran while one was open for 0% of the time, Pallas kernels for 22%

profile of v5, /device:TPU:0, one launch (start us, length us, event | category | flops | bytes accessed | tf_op | source)
XLA Modules:
  0.0 39.8 jit_solution(2641389463475652467)
XLA Ops:
  0.6 1.7 %shard_map.166 = bf16[8,16,1024]{2,1,0:T(8,128)(2,1)} custom-call(bf16[3,32,1024]{2,1,0:T(8,128)(2,1)} %proj_ref.1, bf16[32,1024]{1,0:T(8,128)(2,1)} %cot_ref.1), custom_call_target="tpu_custom_call" | custom-call | tf_op jit(solution)/shard_map/pallas_call | solution.py:615
  2.3 7.3 %all-to-all-start = ((bf16[8,16,1024]{2,1,0:T(8,128)(2,1)}), bf16[8,16,1024]{2,1,0:T(8,128)(2,1)S(1)}, u32[]{:S(2)}, u32[]{:S(2)}) async-start(bf16[8,16,1024]{2,1,0:T(8,128)(2,1)} %shard_map.166), calls=%async_computation | async-start | bytes 524288 | tf_op jit(solution)/shard_map/all_to_all | solution.py:621
  9.6 5.9 %shard_map.165 = (bf16[144,192]{1,0:T(8,128)(2,1)S(1)}, bf16[64,432]{1,0:T(8,128)(2,1)S(1)}, bf16[512,256]{1,0:T(8,128)(2,1)S(1)}, f32[144,128]{1,0:T(8,128)S(1)...) custom-call(bf16[144,192]{1,0:T(8,128)(2,1)} %constant.16.clone.refs, ...), custom_call_target="tpu_custom_call" | custom-call | flops 402653184 | bytes 4194304 | tf_op jit(solution)/shard_map/pallas_call | solution.py:633
  15.5 3.0 %all-to-all-done.refs_0_ = bf16[8,16,1024]{2,1,0:T(8,128)(2,1)S(1)} async-done(((bf16[8,16,1024]{2,1,0:T(8,128)(2,1)}), bf16[8,16,1024]{2,1,0:T(8,128)(2,1)S(1)}, u32[]{:S(2)}, u32[]{:S(2)}) %all-to-all-start) | async-done | bytes 262176 | tf_op jit(solution)/shard_map/all_to_all | solution.py:621
  18.5 3.0 %shard_map.167 = (f32[1024,128]{1,0:T(8,128)S(1)}, f32[8,64,128]{2,1,0:T(8,128)S(1)}, f32[576,256]{1,0:T(8,128)S(1)}, f32[8,8192]{1,0:T(8,128)S(1)}, f32[16,128]...) custom-call(bf16[8,16,1024]{2,1,0:T(8,128)(2,1)S(1)} %all-to-all-done.refs_0_, ...), custom_call_target="tpu_custom_call" | custom-call | flops 419430400 | tf_op jit(solution)/shard_map/pallas_call | solution.py:654
  21.5 1.6 %collective-permute-start = (f32[16,128]{1,0:T(8,128)S(1)}, f32[16,128]{1,0:T(8,128)S(1)}, u32[]{:S(2)}, u32[]{:S(2)}) collective-permute-start(f32[16,128]{1,0:T(8,128)S(1)} %get-tuple-element.46.refs_0_), channel_id=1, source_target_pairs={{0,2},{1,3},{2,0},{3,1},{4,6},{5,7},{6,4},{7,5},{8,10},{9,11},{10,... | collective-permute-start | bytes 24584 | tf_op jit(solution)/shard_map/ppermute | solution.py:688
  23.1 1.9 %shard_map.168.slab_ref = bf16[8,8,2176]{2,1,0:T(8,128)(2,1)S(1)} custom-call(f32[3,3,32]{2,1,0:T(4,128)S(1)} %get-tuple-element.27.refs_9_.short_ref, f32[1024,128]{1,0:T(8,128)S(1)} %get-tuple-element.39.raw_ref, f32[8,64,128]{2,1,0:T(8,128)S(1)} %get-tuple-element.40.mixed_ref, f32[576,256]{1,0:T(8,128)S(1)} %get-tuple-element.41.spec_ref, ...), custom_call_target="tpu_custom_call" | custom-call | flops 419430400 | tf_op jit(solution)/shard_map/pallas_call | solution.py:695
  24.9 0.3 collective-permute-done.refs_1_
  25.2 12.7 %all_to_all.10.recv_ref = bf16[8,8,2176]{2,1,0:T(8,128)(2,1)S(1)} all-to-all(bf16[8,8,2176]{2,1,0:T(8,128)(2,1)S(1)} %shard_map.169), channel_id=1, replica_groups=mesh['seq'=8,'ch'=4] {'seq'}, dimensions={0} | all-to-all | bytes 557056 | tf_op jit(solution)/shard_map/all_to_all | solution.py:722
  37.9 0.1 collective-permute-start.1
  38.0 0.8 %shard_map.170 = (bf16[3,32,1024]{2,1,0:T(8,128)(2,1)}, f32[3,3,32]{2,1,0:T(4,128)}, f32[32,64]{1,0:T(8,128)}) custom-call(bf16[8,8,2176]{2,1,0:T(8,128)(2,1)S(1)} %all_to_all.10.recv_ref), custom_call_target="tpu_custom_call" | custom-call | tf_op jit(solution)/shard_map/pallas_call | solution.py:730
  38.8 0.3 collective-permute-done.1.other_ref
  39.1 0.7 %shard_map.172 = f32[32,64]{1,0:T(8,128)} custom-call(f32[16,128]{1,0:T(8,128)S(1)} %shard_map.171.own_ref, f32[16,128]{1,0:T(8,128)S(1)} %collective-permute-done.1.other_ref), custom_call_target="tpu_custom_call" | custom-call | tf_op jit(solution)/shard_map/pallas_call | solution.py:740
  (2 shorter events, 0.0 us)
Async XLA Ops:
  2.3 16.2 %all-to-all-start = ((bf16[8,16,1024]{2,1,0:T(8,128)(2,1)}), bf16[8,16,1024]{2,1,0:T(8,128)(2,1)S(1)}, u32[]{:S(2)}, u32[]{:S(2)}) async-start(bf16[8,16,1024]{2,1,0:T(8,128)(2,1)} %shard_map.166), calls=%async_computation | async-start | bytes 524288 | tf_op jit(solution)/shard_map/all_to_all | solution.py:621
  21.5 3.7 %collective-permute-start = (f32[16,128]{1,0:T(8,128)S(1)}, f32[16,128]{1,0:T(8,128)S(1)}, u32[]{:S(2)}, u32[]{:S(2)}) collective-permute-start(f32[16,128]{1,0:T(8,128)S(1)} %get-tuple-element.46.refs_0_), channel_id=1, source_target_pairs={{0,2},{1,3},{2,0},{3,1},{4,6},{5,7},{6,4},{7,5},{8,10},{9,11},{10,... | collective-permute-start | bytes 24584 | tf_op jit(solution)/shard_map/ppermute | solution.py:688
  37.9 1.2 %collective-permute-start.1 = (f32[16,128]{1,0:T(8,128)S(1)}, f32[16,128]{1,0:T(8,128)S(1)}, u32[]{:S(2)}, u32[]{:S(2)}) collective-permute-start(f32[16,128]{1,0:T(8,128)S(1)} %shard_map.171.own_ref), channel_id=1, source_target_pairs={{0,1},{1,0},{2,3},{3,2},{4,5},{5,4},{6,7},{7,6},{8,9},{9,8},{10,11... | collective-permute-start | bytes 24584 | tf_op jit(solution)/shard_map/ppermute | solution.py:688

commit v6 on v4

--- a/solution.py
+++ b/solution.py
@@ -92,7 +92,8 @@
     high, low = split(value)
     size = 2 * LANES
     table_high, table_low = middle_ref[:size, :], middle_ref[size:, :]
-    return dot(high, table_high) + dot(high, table_low) + dot(low, table_high)
+    left = jnp.concatenate([high, high, low], 1)
+    return dot(left, jnp.concatenate([table_high, table_low, table_high], 0))
 
 
 def forward(signals, first_ref, middle_ref, turn_ref):
@@ -352,9 +353,7 @@
     for channel in range(per):
         weighted = results[channel] * env_ref[channel * rows : (channel + 1) * rows, :]
         stage_ref[pl.ds(channel, rows, stride=8), :] = weighted
-    out_rows = own_rows(per, out_ref)
-    out_rounded = out_rows.astype(BF16).astype(F32)
-    weights = jnp.concatenate([out_rows, out_rows, out_rows - out_rounded], 0).astype(BF16)
+    out_columns = own_rows(per, out_ref).T
     order, features = out_ref.shape[1], lane_ref.shape[1] // 4
     in_grad_ref[...] = jnp.zeros_like(in_grad_ref)
 
@@ -371,19 +370,24 @@
             parts.append(stage_ref[pl.ds(at, 8), :])
         weighted = jnp.concatenate(parts, 1)
         weighted_ref[:, pl.ds(pl.multiple_of(index * block, LANES), block)] = weighted
-        rounded = weighted.astype(BF16).astype(F32)
-        terms = jnp.concatenate([weighted, weighted - rounded, weighted], 0).astype(BF16)
-        grad = dot_first(weights, terms)
-        high, low = split(grad * cosine_here[...])
-        parts = []
-        for row in range(block_rows):
-            lanes = slice(row * LANES, (row + 1) * LANES)
-            parts.append(jnp.concatenate([high[:, lanes], low[:, lanes]], 1))
-        parts = dot(jnp.concatenate(parts, 0), lane_ref[...])
+        spread = [
+            jnp.broadcast_to(out_columns[:, channel : channel + 1], (order, LANES))
+            for channel in range(per)
+        ]
+        scales = row_ref[pl.ds(pl.multiple_of(index * block_rows, 8), block_rows), :]
         total = jnp.zeros((order, LANES), F32)
-        factors = row_ref[pl.ds(pl.multiple_of(index * block_rows, 8), block_rows), :]
-        for row in range(block_rows):
-            total = total + parts[row * order : (row + 1) * order, :] * factors[row : row + 1, :]
+        for start in range(0, block_rows, 8):
+            parts = []
+            for row in range(start, start + 8):
+                lanes = slice(row * LANES, (row + 1) * LANES)
+                grad = spread[0] * weighted[:1, lanes]
+                for channel in range(1, per):
+                    grad = grad + spread[channel] * weighted[channel : channel + 1, lanes]
+                parts.append(jnp.concatenate(split(grad * cosine_here[:, lanes]), 1))
+            parts = dot(jnp.concatenate(parts, 0), lane_ref[...])
+            for row in range(8):
+                scale = scales[start + row : start + row + 1, :]
+                total = total + parts[row * order : (row + 1) * order, :] * scale
         total = total + pltpu.roll(total, 2 * features, 1)
         total = total + pltpu.roll(total, features, 1)
         total = total.T
@@ -521,9 +525,7 @@
     wide = wide.astype(BF16)
     start, end = slab_ref.shape[2] - (count + 1) * LANES, slab_ref.shape[2] - LANES
     for device in range(slab_ref.shape[0]):
-        result_ref[device, :, :start] = slab_ref[device, :, :start]
         result_ref[device, :, start:end] = wide
-        result_ref[device, :, end:] = slab_ref[device, :, end:]
 
 
 def unpack_kernel(per, recv_ref, proj_ref, short_ref, out_ref):
@@ -704,9 +706,10 @@
     )
     slab = call(
         functools.partial(finish_kernel, scale),
-        sds(shape, BF16),
+        made(shape, BF16),
         limit,
         in_specs=[vmem] * (2 + len(others)),
+        input_output_aliases={0: 0},
     )(put(slab), in_grad, *others)
 
     back = lax.all_to_all(slab, "seq", split_axis=0, concat_axis=0, tiled=True)

time: 40.1 us -> 40.1 us (level)
  no operation moved by 1% of the time
where the time goes in v6:
time: 40.1 us; the launch traced here: 39.8 us
  Pallas kernels  13.9 us (35%)
  blocking collectives  12.7 us (32%)
  starting transfers between devices  8.91 us (22%)
  waiting for transfers between devices  3.63 us (9%)
  between operations  0.66 us (2%)
    all_to_all x1, blocking collectives, shards(): back = lax.all_to_all(slab, 'seq', split_axis=0, concat_axis=0, tiled=True)  12.7 us
    all_to_all x1, starting transfers between devices, shards(): lax.all_to_all(packed, 'seq', split_axis=0, concat_axis=0, tiled=True)  7.25 us
    pallas_call x1, Pallas kernels, shards(): call(functools.partial(filter_kernel, per, length, blocks), tuple((made(v...  5.89 us
    all_to_all x1, waiting for transfers between devices, shards(): lax.all_to_all(packed, 'seq', split_axis=0, concat_axis=0, tiled=True)  3.02 us
    pallas_call x1, Pallas kernels, shards(): call(functools.partial(signal_kernel, per, blocks), (made((rows * step, L...  2.95 us
    pallas_call x1, Pallas kernels, shards(): call(functools.partial(proj_grad_kernel, per, blocks, scale), made(shape,...  1.86 us
    pallas_call x1, Pallas kernels, shards(): call(functools.partial(pack_kernel, per), sds((devices, held, tokens), BF...  1.69 us
    ppermute x2, starting transfers between devices, exchange(): return lax.ppermute(value, 'ch', [(i, i ^ by) for i in range(groups)])  1.66 us
  transfers between devices with their start and end apart: 3, of which 3 were waited for; matrix products, arithmetic and copies ran while one was open for 0% of the time, Pallas kernels for 22%

profile of v6, /device:TPU:0, one launch (start us, length us, event | category | flops | bytes accessed | tf_op | source)
XLA Modules:
  0.0 39.8 jit_solution(11027093279309620785)
XLA Ops:
  0.6 1.7 %shard_map.166 = bf16[8,16,1024]{2,1,0:T(8,128)(2,1)} custom-call(bf16[3,32,1024]{2,1,0:T(8,128)(2,1)} %proj_ref.1, bf16[32,1024]{1,0:T(8,128)(2,1)} %cot_ref.1), custom_call_target="tpu_custom_call" | custom-call | tf_op jit(solution)/shard_map/pallas_call | solution.py:607
  2.3 7.3 %all-to-all-start = ((bf16[8,16,1024]{2,1,0:T(8,128)(2,1)}), bf16[8,16,1024]{2,1,0:T(8,128)(2,1)S(1)}, u32[]{:S(2)}, u32[]{:S(2)}) async-start(bf16[8,16,1024]{2,1,0:T(8,128)(2,1)} %shard_map.166), calls=%async_computation | async-start | bytes 524288 | tf_op jit(solution)/shard_map/all_to_all | solution.py:613
  9.6 5.9 %shard_map.165 = (bf16[144,192]{1,0:T(8,128)(2,1)S(1)}, bf16[64,432]{1,0:T(8,128)(2,1)S(1)}, bf16[512,256]{1,0:T(8,128)(2,1)S(1)}, f32[144,128]{1,0:T(8,128)S(1)...) custom-call(bf16[144,192]{1,0:T(8,128)(2,1)} %constant.16.clone.refs, ...), custom_call_target="tpu_custom_call" | custom-call | flops 402653184 | bytes 4194304 | tf_op jit(solution)/shard_map/pallas_call | solution.py:625
  15.5 3.0 %all-to-all-done.refs_0_ = bf16[8,16,1024]{2,1,0:T(8,128)(2,1)S(1)} async-done(((bf16[8,16,1024]{2,1,0:T(8,128)(2,1)}), bf16[8,16,1024]{2,1,0:T(8,128)(2,1)S(1)}, u32[]{:S(2)}, u32[]{:S(2)}) %all-to-all-start) | async-done | bytes 262176 | tf_op jit(solution)/shard_map/all_to_all | solution.py:613
  18.5 2.9 %shard_map.167 = (f32[1024,128]{1,0:T(8,128)S(1)}, f32[8,64,128]{2,1,0:T(8,128)S(1)}, f32[576,256]{1,0:T(8,128)S(1)}, f32[8,8192]{1,0:T(8,128)S(1)}, f32[16,128]...) custom-call(bf16[8,16,1024]{2,1,0:T(8,128)(2,1)S(1)} %all-to-all-done.refs_0_, ...), custom_call_target="tpu_custom_call" | custom-call | flops 419430400 | tf_op jit(solution)/shard_map/pallas_call | solution.py:646
  21.5 1.6 %collective-permute-start = (f32[16,128]{1,0:T(8,128)S(1)}, f32[16,128]{1,0:T(8,128)S(1)}, u32[]{:S(2)}, u32[]{:S(2)}) collective-permute-start(f32[16,128]{1,0:T(8,128)S(1)} %get-tuple-element.46.refs_0_), channel_id=1, source_target_pairs={{0,2},{1,3},{2,0},{3,1},{4,6},{5,7},{6,4},{7,5},{8,10},{9,11},{10,... | collective-permute-start | bytes 24584 | tf_op jit(solution)/shard_map/ppermute | solution.py:680
  23.0 1.9 %shard_map.168.slab_ref = bf16[8,8,2176]{2,1,0:T(8,128)(2,1)S(1)} custom-call(f32[3,3,32]{2,1,0:T(4,128)S(1)} %get-tuple-element.27.refs_9_.short_ref, f32[1024,128]{1,0:T(8,128)S(1)} %get-tuple-element.39.raw_ref, f32[8,64,128]{2,1,0:T(8,128)S(1)} %get-tuple-element.40.mixed_ref, f32[576,256]{1,0:T(8,128)S(1)} %get-tuple-element.41.spec_ref, ...), custom_call_target="tpu_custom_call" | custom-call | flops 419430400 | tf_op jit(solution)/shard_map/pallas_call | solution.py:687
  24.9 0.3 collective-permute-done.refs_1_
  25.2 12.7 %all_to_all.10.recv_ref = bf16[8,8,2176]{2,1,0:T(8,128)(2,1)S(1)} all-to-all(bf16[8,8,2176]{2,1,0:T(8,128)(2,1)S(1)} %shard_map.169), channel_id=1, replica_groups=mesh['seq'=8,'ch'=4] {'seq'}, dimensions={0} | all-to-all | bytes 557056 | tf_op jit(solution)/shard_map/all_to_all | solution.py:715
  37.9 0.1 collective-permute-start.1
  37.9 0.8 %shard_map.170 = (bf16[3,32,1024]{2,1,0:T(8,128)(2,1)}, f32[3,3,32]{2,1,0:T(4,128)}, f32[32,64]{1,0:T(8,128)}) custom-call(bf16[8,8,2176]{2,1,0:T(8,128)(2,1)S(1)} %all_to_all.10.recv_ref), custom_call_target="tpu_custom_call" | custom-call | tf_op jit(solution)/shard_map/pallas_call | solution.py:723
  38.7 0.3 collective-permute-done.1.other_ref
  39.1 0.7 %shard_map.172 = f32[32,64]{1,0:T(8,128)} custom-call(f32[16,128]{1,0:T(8,128)S(1)} %shard_map.171.own_ref, f32[16,128]{1,0:T(8,128)S(1)} %collective-permute-done.1.other_ref), custom_call_target="tpu_custom_call" | custom-call | tf_op jit(solution)/shard_map/pallas_call | solution.py:733
  (2 shorter events, 0.0 us)
Async XLA Ops:
  2.3 16.2 %all-to-all-start = ((bf16[8,16,1024]{2,1,0:T(8,128)(2,1)}), bf16[8,16,1024]{2,1,0:T(8,128)(2,1)S(1)}, u32[]{:S(2)}, u32[]{:S(2)}) async-start(bf16[8,16,1024]{2,1,0:T(8,128)(2,1)} %shard_map.166), calls=%async_computation | async-start | bytes 524288 | tf_op jit(solution)/shard_map/all_to_all | solution.py:613
  21.5 3.7 %collective-permute-start = (f32[16,128]{1,0:T(8,128)S(1)}, f32[16,128]{1,0:T(8,128)S(1)}, u32[]{:S(2)}, u32[]{:S(2)}) collective-permute-start(f32[16,128]{1,0:T(8,128)S(1)} %get-tuple-element.46.refs_0_), channel_id=1, source_target_pairs={{0,2},{1,3},{2,0},{3,1},{4,6},{5,7},{6,4},{7,5},{8,10},{9,11},{10,... | collective-permute-start | bytes 24584 | tf_op jit(solution)/shard_map/ppermute | solution.py:680
  37.9 1.2 %collective-permute-start.1 = (f32[16,128]{1,0:T(8,128)S(1)}, f32[16,128]{1,0:T(8,128)S(1)}, u32[]{:S(2)}, u32[]{:S(2)}) collective-permute-start(f32[16,128]{1,0:T(8,128)S(1)} %shard_map.171.own_ref), channel_id=1, source_target_pairs={{0,1},{1,0},{2,3},{3,2},{4,5},{5,4},{6,7},{7,6},{8,9},{9,8},{10,11... | collective-permute-start | bytes 24584 | tf_op jit(solution)/shard_map/ppermute | solution.py:680
